TPU v7x, 32 devices: a whole 2x2x4 slice. The times are simulated.
32 devices in a mesh: au: 4 (over y, x), vert: 4 (over z), af: 2 (over core).
Axes of the slice: x: 2, y: 2, z: 4, core: 2. Of those that a mesh axis runs over, the one named last changes fastest.
Arguments:
- visib: float32 [2, 256, 1024], P('af', ('au', 'vert')), may hold values from -6 to 6
- coords: float32 [2, 256, 1024], P('af', ('au', 'vert')), may hold values from -16 to 16
- owner: int32 [2, 256], P('af', ('au', 'vert')), may hold values from 0 to 15, as said below
- offsets: int32 [2, 256, 2], P('af', ('au', 'vert')), may hold values from 0 to 448
- stations: int32 [2, 256, 2], P('af', ('au', 'vert')), may hold values from 0 to 511, as said below
- live: int32 [2, 16], P('af', ('au', 'vert')), may hold values from 16 to 16, as said below
- beams: bfloat16 [2, 512, 8192], P('af', ('au', 'vert')), may hold values from -4.1875 to 4.1875
- taper: float32 [2048, 2048], P('au', 'vert'), may hold values from 0.5 to 2
Outputs:
- predicted: float32 [2, 256, 1024], P('af', ('au', 'vert'))
- model_grid: float32 [2, 2048, 2048], P(None, 'au', 'vert')
Inputs may be any that keep to these rules, and one draw needn't show every extreme that they name: A tile id is tile row times the number of tile columns plus tile column. The owner of a live block is its holder's tile or one of the eight tiles around it inside the grid; the owner of a dead block is its holder's tile. Among the live blocks of one holder, at most 2 name any one other tile, and in every channel group one tile receives exactly 2 blocks from each of its eight neighbours. The two stations of a block differ. Counting both stations of all 16 blocks of one holder, at most 4 of these entries lie on the stations s of any one value of s // 32, and some value takes exactly 4 on every holder. In every channel group some holder has all 16 blocks live.
All inputs are finite; a program needn't handle non-finite values.
Results may differ from a plain program's by a relative error of at most 0.0004.
Values may be sent and summed in bfloat16 or wider, within the bound.
A program may use at most 64 MiB of HBM per device.

v0:
```python
import math

import jax
import jax.numpy as jnp
from jax import lax
from jax.sharding import PartitionSpec as P

S = 64
CAP = 2
NB = 16
TS = 512


highest = lax.Precision.HIGHEST


def shifted(value, axis, steps):
    count = lax.axis_size(axis)
    leading, last = (max(0, -steps), min(count, count - steps))
    return lax.ppermute(value, axis, [(source, source + steps) for source in range(leading, last)])


def tables(side_len):
    positions = jnp.arange(side_len, dtype=jnp.int32)
    wrapped = positions[:, None] * positions[None, :] % side_len
    angles = wrapped.astype(jnp.float32) * (2.0 * math.pi / side_len)
    scaling = 1.0 / math.sqrt(side_len)
    return (jnp.cos(angles) * scaling, -jnp.sin(angles) * scaling)


def rotate(values):
    half_width = values.shape[-1] // 2
    return jnp.concatenate([-values[..., half_width:], values[..., :half_width]], axis=-1)


def complex_mul(values, factor):
    half_width = values.shape[-1] // 2
    x_real, x_imag = (values[..., :half_width], values[..., half_width:])
    a_real, a_imag = (factor[..., :half_width], factor[..., half_width:])
    return jnp.concatenate(
        [x_real * a_real - x_imag * a_imag, x_real * a_imag + x_imag * a_real], axis=-1
    )


def conj_mul(values, factor):
    half_width = values.shape[-1] // 2
    x_real, x_imag = (values[..., :half_width], values[..., half_width:])
    a_real, a_imag = (factor[..., :half_width], factor[..., half_width:])
    return jnp.concatenate(
        [x_real * a_real + x_imag * a_imag, x_imag * a_real - x_real * a_imag], axis=-1
    )


def phases(coords_in, side_len):
    centre = jnp.arange(side_len, dtype=jnp.float32) - side_len / 2
    angles = coords_in[..., None] * centre * (2.0 * math.pi / side_len)
    return (jnp.cos(angles), jnp.sin(angles))


def grid_blocks(visib_rows, coord_rows, beam_terms):
    row_count = visib_rows.shape[-1] // 2
    side_len = beam_terms.shape[-2]
    cos_u, sin_u = phases(coord_rows[..., :row_count], side_len)
    cos_v, sin_v = phases(coord_rows[..., row_count:], side_len)
    vis_real = visib_rows[..., :row_count, None]
    vis_imag = visib_rows[..., row_count:, None]
    weighted = jnp.concatenate(
        [vis_real * cos_v - vis_imag * sin_v, vis_real * sin_v + vis_imag * cos_v], axis=-1
    )
    first = jnp.einsum("krl,krc->klc", cos_u, weighted, precision=highest)
    second = jnp.einsum("krl,krc->klc", sin_u, weighted, precision=highest)
    image_part = (first + rotate(second)) * (1.0 / math.sqrt(row_count))
    image_part = complex_mul(image_part, beam_terms)
    table_real, table_imag = tables(side_len)
    left_side = jnp.einsum("al,klc->kac", table_real, image_part, precision=highest)
    left_side = left_side + rotate(
        jnp.einsum("al,klc->kac", table_imag, image_part, precision=highest)
    )
    right_side = jnp.concatenate(
        [
            jnp.concatenate([table_real, table_imag], 1),
            jnp.concatenate([-table_imag, table_real], 1),
        ],
        0,
    )
    return jnp.einsum("kac,cd->kad", left_side, right_side, precision=highest)


def degrid_blocks(windows, coord_rows, beam_terms):
    side_len = windows.shape[-2]
    row_count = coord_rows.shape[-1] // 2
    table_real, table_imag = tables(side_len)
    left_side = jnp.einsum("al,klc->kac", table_real, windows, precision=highest)
    left_side = left_side - rotate(
        jnp.einsum("al,klc->kac", table_imag, windows, precision=highest)
    )
    right_side = jnp.concatenate(
        [
            jnp.concatenate([table_real, -table_imag], 1),
            jnp.concatenate([table_imag, table_real], 1),
        ],
        0,
    )
    image_part = jnp.einsum("kac,cd->kad", left_side, right_side, precision=highest)
    image_part = conj_mul(image_part, beam_terms)
    cos_u, sin_u = phases(coord_rows[..., :row_count], side_len)
    cos_v, sin_v = phases(coord_rows[..., row_count:], side_len)
    first = jnp.einsum("krl,klc->krc", cos_u, image_part, precision=highest)
    second = jnp.einsum("krl,klc->krc", sin_u, image_part, precision=highest)
    along_rows = first - rotate(second)
    a_real = along_rows[..., :side_len]
    a_imag = along_rows[..., side_len:]
    real_part = jnp.sum(a_real * cos_v + a_imag * sin_v, axis=-1)
    imag_part = jnp.sum(a_imag * cos_v - a_real * sin_v, axis=-1)
    return jnp.concatenate([real_part, imag_part], axis=-1) * (1.0 / side_len)


def body(visib, coords, owner, offsets, stations, live, beams, taper):
    n_vert = lax.axis_size("vert")
    my_row = lax.axis_index("au")
    my_col = lax.axis_index("vert")
    signal = visib[0]
    places = coords[0]
    owners = owner[0]
    shifts_in = offsets[0]
    pair_ids = stations[0]
    beam_rows = beams[0]
    sig_width = signal.shape[1]
    held_slot = jnp.arange(NB, dtype=jnp.int32)
    is_alive = held_slot < live[0, 0]
    heading = (owners // n_vert - my_row + 1) * 3 + (owners % n_vert - my_col + 1)
    heading = jnp.where(is_alive, heading, 4)
    order_in = jnp.sum(
        ((heading[:, None] == heading[None, :]) & (held_slot[None, :] < held_slot[:, None])).astype(
            jnp.int32
        ),
        axis=1,
    )
    route_ids = jnp.arange(9, dtype=jnp.int32)
    cap_slots = jnp.arange(CAP, dtype=jnp.int32)
    route_hit = (heading[None, None, :] == route_ids[:, None, None]) & (
        order_in[None, None, :] == cap_slots[None, :, None]
    )
    picked = jnp.sum(jnp.where(route_hit, held_slot[None, None, :], 0), axis=2)
    filled = jnp.any(route_hit, axis=2).astype(jnp.int32)
    row_data = jnp.concatenate([signal, places], axis=1)
    int_rows = jnp.concatenate([shifts_in, pair_ids], axis=1)
    send_floats = jnp.take(row_data, picked, axis=0) * filled[..., None].astype(jnp.float32)
    send_ints = jnp.concatenate([jnp.take(int_rows, picked, axis=0), filled[..., None]], axis=-1)
    self_mask = (is_alive & (heading == 4)).astype(jnp.int32)
    float_parts = [row_data * self_mask[:, None].astype(jnp.float32)]
    int_parts = [jnp.concatenate([int_rows, self_mask[:, None]], axis=1)]
    for route_id in range(9):
        if route_id != 4:
            move_by = (route_id // 3 - 1) * n_vert + (route_id % 3 - 1)
            arrived_floats, arrived_ints = shifted(
                (send_floats[route_id], send_ints[route_id]), ("au", "vert"), move_by
            )
            float_parts.append(arrived_floats)
            int_parts.append(arrived_ints)
    slot_floats = jnp.concatenate(float_parts, axis=0)
    slot_ints = jnp.concatenate(int_parts, axis=0)
    slot_count = slot_floats.shape[0]
    slot_signal = slot_floats[:, :sig_width]
    slot_places = slot_floats[:, sig_width : 2 * sig_width]
    present = slot_ints[:, 4].astype(jnp.float32)
    wanted_ids = jnp.concatenate([slot_ints[:, 2], slot_ints[:, 3]], axis=0)
    piece_rows = lax.all_gather(beam_rows, ("au", "vert"), axis=0, tiled=True)
    station_ids = jnp.arange(piece_rows.shape[0], dtype=jnp.int32)
    one_hot = (wanted_ids[:, None] == station_ids[None, :]).astype(jnp.bfloat16)
    found_rows = jnp.dot(one_hot, piece_rows, preferred_element_type=jnp.float32)
    beam_terms = conj_mul(
        found_rows[:slot_count].reshape(slot_count, S, 2 * S),
        found_rows[slot_count:].reshape(slot_count, S, 2 * S),
    )
    subgrids = grid_blocks(slot_signal, slot_places, beam_terms) * present[:, None, None]
    rows_at = slot_ints[:, 0]
    cols_at = slot_ints[:, 1]
    zero_index = jnp.zeros((), jnp.int32)

    def add_one(slot_at, partial_value):
        subgrid = subgrids[slot_at].reshape(S, 2, S).transpose(1, 0, 2)
        corner = (zero_index, rows_at[slot_at], cols_at[slot_at])
        window = lax.dynamic_slice(partial_value, corner, (2, S, S))
        return lax.dynamic_update_slice(partial_value, window + subgrid, corner)

    tile_sum = lax.fori_loop(0, slot_count, add_one, jnp.zeros((2, TS, TS), jnp.float32))
    model_grid = lax.psum(tile_sum, "af") * taper[None]

    def cut_window(row_at, col_at):
        return lax.dynamic_slice(model_grid, (zero_index, row_at, col_at), (2, S, S))

    windows = jax.vmap(cut_window)(rows_at, cols_at)
    windows = jnp.transpose(windows, (0, 2, 1, 3)).reshape(slot_count, S, 2 * S)
    guesses = degrid_blocks(windows, slot_places, beam_terms)
    own_guess = guesses[:NB]
    returned = []
    slot_at = NB
    for route_id in range(9):
        if route_id == 4:
            returned.append(jnp.zeros((CAP, guesses.shape[1]), jnp.float32))
        else:
            move_by = (route_id // 3 - 1) * n_vert + (route_id % 3 - 1)
            block_part = guesses[slot_at : slot_at + CAP]
            slot_at = slot_at + CAP
            returned.append(shifted(block_part, ("au", "vert"), -move_by))
    stacked = jnp.stack(returned, axis=0).reshape(9 * CAP, guesses.shape[1])
    lookup = heading * CAP + jnp.minimum(order_in, CAP - 1)
    remote = jnp.take(stacked, lookup, axis=0)
    result = jnp.where((heading == 4)[:, None], own_guess, remote) * is_alive[:, None].astype(
        jnp.float32
    )
    return (result[None], model_grid)


def solution(mesh):
    placed = (
        P("af", ("au", "vert"), None),
        P("af", ("au", "vert"), None),
        P("af", ("au", "vert")),
        P("af", ("au", "vert"), None),
        P("af", ("au", "vert"), None),
        P("af", ("au", "vert")),
        P("af", ("au", "vert"), None),
        P("au", "vert"),
    )
    return jax.shard_map(
        body,
        mesh=mesh,
        in_specs=placed,
        out_specs=(P("af", ("au", "vert"), None), P(None, "au", "vert")),
        check_vma=False,
    )
```

profile of v0, /device:TPU:9, one launch (start us, length us, event | category | flops | bytes accessed | tf_op | source)
XLA Modules:
  0.0 722.4 jit_solution(3955062832411697185)
XLA Ops:
  23.9 4.7 collective-permute-done.10
  30.5 2.6 collective-permute-done.11
  35.0 2.4 collective-permute-done.12
  37.4 8.0 %collective-permute-start.13 = (s32[2,5]{0,1:T(8,128)S(1)}, s32[2,5]{0,1:T(8,128)S(1)}, u32[]{:S(2)}, u32[]{:S(2)}) collective-permute-start(s32[2,5]{0,1:T(8,128)S(1)} %copy.113), channel_id=1, source_target_pairs={{0,6},{2,8},{4,10},{6,12},{8,14},{10,16},{12,18},{14,20},{16,22},{... | collective-permute-start | bytes 128 | tf_op jit(solution)/shard_map/ppermute | solution.py:20
  46.1 5.9 collective-permute-start.14
  52.8 3.9 collective-permute-start.15
  58.7 6.3 collective-permute-done.8
  66.3 4.1 collective-permute-done.9
  70.4 3.5 collective-permute-start.4
  74.6 5.1 collective-permute-start.5
  79.7 3.4 collective-permute-start.6
  86.0 15.6 %multiply_subtract_fusion = (f32[32,512,64]{1,2,0:T(8,128)S(1)}, f32[32,512,64]{1,2,0:T(8,128)S(1)}) fusion(f32[32,512]{1,0:T(8,128)S(1)} %get-tuple-element.147, f32[32,512]{1,0:T(8,128)S(1)} %get-tuple-element.148, f32[32,512]{1,0:T(8,128)S(1)} %get-tuple-element.146, f32[64]{0:T(128)S(1)} %iota_add_fusion), kind=kLoop, calls=%fused_computation.18 | loop fusion | flops 8388608 | bytes 8585472 | tf_op jit(solution)/shard_map/sub | solution.py:68
  101.6 23.1 %fusion.2 = f32[32,64,128]{2,1,0:T(8,128)S(1)} fusion(f32[32,512,64]{1,2,0:T(8,128)S(1)} %get-tuple-element.151, f32[32,512,64]{1,2,0:T(8,128)S(1)} %get-tuple-element.150, f32[64]{0:T(128)S(1)} %iota_add_fusion, f32[32,512]{1,0:T(8,128)S(1)} %get-tuple-element.149), kind=kOutput, calls=%fused_computation.12 | convolution fusion | flops 1614807040 | bytes 9502976 | tf_op jit(solution)/shard_map/krl,krc->klc/dot_general | solution.py:71
  125.0 34.2 %fusion.33 = f32[32,64,128]{2,1,0:T(8,128)S(1)} fusion(f32[32,512,64]{1,2,0:T(8,128)S(1)} %get-tuple-element.151, f32[32,512,64]{1,2,0:T(8,128)S(1)} %get-tuple-element.150, f32[64]{0:T(128)S(1)} %iota_add_fusion, f32[32,512]{1,0:T(8,128)S(1)} %get-tuple-element.149, f32[32,64,64]{2,1,0:T(8,128)S(1)} %get-tuple-element.145, ...), kind=kOutput, calls=%fused_computation.46 | convolution fusion | flops 1615593472 | bytes 10551552 | tf_op jit(solution)/shard_map/krl,krc->klc/dot_general | solution.py:70
  159.2 5.0 fusion
  171.9 304.1 %while.14 = (s32[]{:T(128)}, f32[2,512,512]{2,1,0:T(8,128)S(1)}, s32[32]{0:T(128)}, s32[32]{0:T(128)}, f32[32,64,128]{2,1,0:T(8,128)}, /*index=5*/s32[]{:T(128)}, s32[]{:T(128)}, s32[]{:T(128)}) while((s32[]{:T(128)}, f32[2,512,512]{2,1,0:T(8,128)S(1)}, s32[32]{0:T(128)}, s32[32]{0:T(128)}, f32[32,64,128]{2,1,0:T(8,128)}, ...), condition=%wide.region_4.5_spmd, body=%wide.region_3.4_spmd.sunk | while | flops 8200 | bytes 426177 | solution.py:187
  478.0 38.2 %all-reduce.2.cloned.1.call-done = f32[2,512,512]{2,1,0:T(8,128)} async-done(((f32[2,512,512]{2,1,0:T(8,128)}), f32[2,512,512]{2,1,0:T(8,128)}) %all-reduce.2.cloned.1.call-update) | async-done | bytes 2097168 | tf_op jit(solution)/shard_map/psum | solution.py:188
  516.2 2.2 broadcast_multiply_fusion
  518.4 86.2 %while.15 = (s32[]{:T(128)}, f32[2,512,512]{2,1,0:T(8,128)S(1)}, s32[32,3]{0,1:T(4,128)S(1)}, f32[32,2,64,64]{3,2,1,0:T(8,128)}, s32[]{:T(128)}) while((s32[]{:T(128)}, f32[2,512,512]{2,1,0:T(8,128)S(1)}, s32[32,3]{0,1:T(4,128)S(1)}, f32[32,2,64,64]{3,2,1,0:T(8,128)}, s32[]{:T(128)}) %tuple.95), condition=%wide.while_cond, body=%wide.while_body.sunk | while | flops 2 | bytes 99945 | solution.py:191
  519.1 2.0 bitcast_dynamic-update-slice_fusion.2
  527.1 2.0 bitcast_dynamic-update-slice_fusion.2
  529.8 2.0 bitcast_dynamic-update-slice_fusion.2
  532.5 2.0 bitcast_dynamic-update-slice_fusion.2
  540.6 2.0 bitcast_dynamic-update-slice_fusion.2
  548.7 2.0 bitcast_dynamic-update-slice_fusion.2
  551.4 2.0 bitcast_dynamic-update-slice_fusion.2
  559.5 2.0 bitcast_dynamic-update-slice_fusion.2
  564.8 2.0 bitcast_dynamic-update-slice_fusion.2
  567.5 2.0 bitcast_dynamic-update-slice_fusion.2
  570.2 2.0 bitcast_dynamic-update-slice_fusion.2
  572.9 2.0 bitcast_dynamic-update-slice_fusion.2
  575.6 2.0 bitcast_dynamic-update-slice_fusion.2
  578.3 2.0 bitcast_dynamic-update-slice_fusion.2
  586.4 2.0 bitcast_dynamic-update-slice_fusion.2
  591.8 2.0 bitcast_dynamic-update-slice_fusion.2
  597.2 2.0 bitcast_dynamic-update-slice_fusion.2
  605.9 4.6 copy.119
  610.5 2.6 reshape.416
  617.8 25.5 %fusion.11 = f32[32,512,128]{1,2,0:T(8,128)S(1)} fusion(f32[64]{0:T(128)S(1)} %iota_add_fusion, f32[32,512]{1,0:T(8,128)S(1)} %get-tuple-element.149, f32[32,64,64]{2,1,0:T(8,128)S(1)} %get-tuple-element.137, f32[32,64,64]{2,1,0:T(8,128)S(1)} %get-tuple-element.136), kind=kOutput, calls=%fused_computation.26 | convolution fusion | flops 1612972032 | bytes 9502976 | tf_op jit(solution)/shard_map/krl,klc->krc/dot_general | solution.py:109
  645.2 25.7 %maximum_subtract_fusion = f32[32,512,128]{1,2,0:T(8,128)S(1)} fusion(f32[32,512,64]{1,2,0:T(8,128)S(1)} %get-tuple-element.135, f32[32,512,64]{1,2,0:T(8,128)S(1)} %get-tuple-element.134, f32[64]{0:T(128)S(1)} %iota_add_fusion, f32[32,512]{1,0:T(8,128)S(1)} %get-tuple-element.149, f32[32,64,64]{2,1,0:T(8,128)S(1)} %get-tuple-element.137, ...), kind=kOutput, calls=%fused_computation.9 | convolution fusion | flops 1617166336 | bytes 17891584 | tf_op jit(solution)/shard_map/krl,klc->krc/dot_general | solution.py:108
  670.9 17.4 %add_reduce_fusion = (f32[32,512]{1,0:T(8,128)S(1)}, f32[32,512]{1,0:T(8,128)S(1)}) fusion(f32[32,512,128]{1,2,0:T(8,128)S(1)} %maximum_subtract_fusion, f32[32,512]{1,0:T(8,128)S(1)} %get-tuple-element.148, f32[64]{0:T(128)S(1)} %iota_add_fusion), kind=kLoop, calls=%fused_computation.16 | loop fusion | flops 10452992 | bytes 8585472 | tf_op jit(solution)/shard_map/reduce_sum | solution.py:113
  688.3 4.0 collective-permute-start.16
  692.3 3.1 collective-permute-start.17
  695.4 3.1 collective-permute-start.18
  698.5 3.1 collective-permute-start.19
  701.6 2.2 collective-permute-start.20
  707.8 2.5 collective-permute-done.21
  711.1 2.9 collective-permute-done.23
  (461 shorter events, 273.1 us)
Async XLA Ops:
  7.2 152.1 %all-gather.3.cloned.1.call-start = ((), (), s32[]{:S(2)}) async-start(), calls=%async_computation.1 | async-start | bytes 8912896 | tf_op jit(solution)/shard_map/all_gather | solution.py:168
  7.9 508.3 %all-reduce.2.cloned.1.call-start = ((), (), s32[]{:S(2)}) async-start(), calls=%async_computation | async-start | bytes 4194304 | tf_op jit(solution)/shard_map/psum | solution.py:188
  12.6 61.9 %collective-permute-start = (f32[2,2048]{1,0:T(2,128)S(1)}, f32[2,2048]{1,0:T(2,128)S(1)}, u32[]{:S(2)}, u32[]{:S(2)}) collective-permute-start(f32[2,2048]{1,0:T(2,128)S(1)} %get-tuple-element.159), channel_id=1, source_target_pairs={{10,0},{12,2},{14,4},{16,6},{18,8},{20,10},{22,12},{24,14},{26,16}... | collective-permute-start | bytes 49160 | tf_op jit(solution)/shard_map/ppermute | solution.py:20
  13.9 65.7 %collective-permute-start.1 = (f32[2,2048]{1,0:T(2,128)S(1)}, f32[2,2048]{1,0:T(2,128)S(1)}, u32[]{:S(2)}, u32[]{:S(2)}) collective-permute-start(f32[2,2048]{1,0:T(2,128)S(1)} %get-tuple-element.158), channel_id=1, source_target_pairs={{8,0},{10,2},{12,4},{14,6},{16,8},{18,10},{20,12},{22,14},{24,16},... | collective-permute-start | bytes 49160 | tf_op jit(solution)/shard_map/ppermute | solution.py:20
  15.2 67.8 %collective-permute-start.2 = (f32[2,2048]{1,0:T(2,128)S(1)}, f32[2,2048]{1,0:T(2,128)S(1)}, u32[]{:S(2)}, u32[]{:S(2)}) collective-permute-start(f32[2,2048]{1,0:T(2,128)S(1)} %get-tuple-element.157), channel_id=1, source_target_pairs={{6,0},{8,2},{10,4},{12,6},{14,8},{16,10},{18,12},{20,14},{22,16},{... | collective-permute-start | bytes 49160 | tf_op jit(solution)/shard_map/ppermute | solution.py:20
  16.5 68.5 %collective-permute-start.3 = (f32[2,2048]{1,0:T(2,128)S(1)}, f32[2,2048]{1,0:T(2,128)S(1)}, u32[]{:S(2)}, u32[]{:S(2)}) collective-permute-start(f32[2,2048]{1,0:T(2,128)S(1)} %get-tuple-element.156), channel_id=1, source_target_pairs={{2,0},{4,2},{6,4},{8,6},{10,8},{12,10},{14,12},{16,14},{18,16},{20... | collective-permute-start | bytes 49160 | tf_op jit(solution)/shard_map/ppermute | solution.py:20
  20.2 8.4 %collective-permute-start.10 = (s32[2,5]{0,1:T(8,128)S(1)}, s32[2,5]{0,1:T(8,128)S(1)}, u32[]{:S(2)}, u32[]{:S(2)}) collective-permute-start(s32[2,5]{0,1:T(8,128)S(1)} %copy.110), channel_id=1, source_target_pairs={{6,0},{8,2},{10,4},{12,6},{14,8},{16,10},{18,12},{20,14},{22,16},{... | collective-permute-start | bytes 128 | tf_op jit(solution)/shard_map/ppermute | solution.py:20
  28.6 4.5 collective-permute-start.11
  33.1 4.3 collective-permute-start.12
  37.4 8.7 %collective-permute-start.13 = (s32[2,5]{0,1:T(8,128)S(1)}, s32[2,5]{0,1:T(8,128)S(1)}, u32[]{:S(2)}, u32[]{:S(2)}) collective-permute-start(s32[2,5]{0,1:T(8,128)S(1)} %copy.113), channel_id=1, source_target_pairs={{0,6},{2,8},{4,10},{6,12},{8,14},{10,16},{12,18},{14,20},{16,22},{... | collective-permute-start | bytes 128 | tf_op jit(solution)/shard_map/ppermute | solution.py:20
  46.1 6.7 collective-permute-start.14
  52.8 4.7 collective-permute-start.15
  57.4 7.6 %collective-permute-start.8 = (s32[2,5]{0,1:T(8,128)S(1)}, s32[2,5]{0,1:T(8,128)S(1)}, u32[]{:S(2)}, u32[]{:S(2)}) collective-permute-start(s32[2,5]{0,1:T(8,128)S(1)} %copy.108), channel_id=1, source_target_pairs={{10,0},{12,2},{14,4},{16,6},{18,8},{20,10},{22,12},{24,14},{26,16}... | collective-permute-start | bytes 128 | tf_op jit(solution)/shard_map/ppermute | solution.py:20
  65.0 5.4 collective-permute-start.9
  70.4 14.7 %collective-permute-start.4 = (f32[2,2048]{1,0:T(2,128)S(1)}, f32[2,2048]{1,0:T(2,128)S(1)}, u32[]{:S(2)}, u32[]{:S(2)}) collective-permute-start(f32[2,2048]{1,0:T(2,128)S(1)} %get-tuple-element.155), channel_id=1, source_target_pairs={{0,2},{2,4},{4,6},{6,8},{8,10},{10,12},{12,14},{14,16},{16,18},{18... | collective-permute-start | bytes 49160 | tf_op jit(solution)/shard_map/ppermute | solution.py:20
  74.6 10.5 %collective-permute-start.5 = (f32[2,2048]{1,0:T(2,128)S(1)}, f32[2,2048]{1,0:T(2,128)S(1)}, u32[]{:S(2)}, u32[]{:S(2)}) collective-permute-start(f32[2,2048]{1,0:T(2,128)S(1)} %get-tuple-element.154), channel_id=1, source_target_pairs={{0,6},{2,8},{4,10},{6,12},{8,14},{10,16},{12,18},{14,20},{16,22},{... | collective-permute-start | bytes 49160 | tf_op jit(solution)/shard_map/ppermute | solution.py:20
  79.7 5.4 collective-permute-start.6
  83.1 2.7 collective-permute-start.7
  165.7 1.8 copy-start.1
  476.0 1.3 copy-start
  604.6 1.3 copy-start.3
  614.7 2.4 copy-start.2
  688.3 15.5 %collective-permute-start.16 = (f32[2,1024]{1,0:T(2,128)S(1)}, f32[2,1024]{1,0:T(2,128)S(1)}, u32[]{:S(2)}, u32[]{:S(2)}) collective-permute-start(f32[2,1024]{1,0:T(2,128)S(1)} %get-tuple-element.167), channel_id=1, source_target_pairs={{0,10},{2,12},{4,14},{6,16},{8,18},{10,20},{12,22},{14,24},{16,26}... | collective-permute-start | bytes 24584 | tf_op jit(solution)/shard_map/ppermute | solution.py:20
  692.3 12.8 %collective-permute-start.17 = (f32[2,1024]{1,0:T(2,128)S(1)}, f32[2,1024]{1,0:T(2,128)S(1)}, u32[]{:S(2)}, u32[]{:S(2)}) collective-permute-start(f32[2,1024]{1,0:T(2,128)S(1)} %get-tuple-element.166), channel_id=1, source_target_pairs={{0,8},{2,10},{4,12},{6,14},{8,16},{10,18},{12,20},{14,22},{16,24},... | collective-permute-start | bytes 24584 | tf_op jit(solution)/shard_map/ppermute | solution.py:20
  695.4 11.0 %collective-permute-start.18 = (f32[2,1024]{1,0:T(2,128)S(1)}, f32[2,1024]{1,0:T(2,128)S(1)}, u32[]{:S(2)}, u32[]{:S(2)}) collective-permute-start(f32[2,1024]{1,0:T(2,128)S(1)} %get-tuple-element.165), channel_id=1, source_target_pairs={{0,6},{2,8},{4,10},{6,12},{8,14},{10,16},{12,18},{14,20},{16,22},{... | collective-permute-start | bytes 24584 | tf_op jit(solution)/shard_map/ppermute | solution.py:20
  698.5 9.3 %collective-permute-start.19 = (f32[2,1024]{1,0:T(2,128)S(1)}, f32[2,1024]{1,0:T(2,128)S(1)}, u32[]{:S(2)}, u32[]{:S(2)}) collective-permute-start(f32[2,1024]{1,0:T(2,128)S(1)} %get-tuple-element.164), channel_id=1, source_target_pairs={{0,2},{2,4},{4,6},{6,8},{8,10},{10,12},{12,14},{14,16},{16,18},{18... | collective-permute-start | bytes 24584 | tf_op jit(solution)/shard_map/ppermute | solution.py:20
  701.6 6.2 collective-permute-start.20
  703.8 6.5 collective-permute-start.21
  705.1 5.9 collective-permute-start.22
  706.5 7.5 %collective-permute-start.23 = (f32[2,1024]{1,0:T(2,128)S(1)}, f32[2,1024]{1,0:T(2,128)S(1)}, u32[]{:S(2)}, u32[]{:S(2)}) collective-permute-start(f32[2,1024]{1,0:T(2,128)S(1)} %get-tuple-element.160), channel_id=1, source_target_pairs={{10,0},{12,2},{14,4},{16,6},{18,8},{20,10},{22,12},{24,14},{26,16}... | collective-permute-start | bytes 24584 | tf_op jit(solution)/shard_map/ppermute | solution.py:20
Sparse Core Ops, SparseCore 0:
  10.8 113.8 all-gather.2
  477.5 38.6 all-reduce.1
where the time goes:
time: 737 us; the launch traced here: 722 us
  local copies, waits for them, and re-layouts  268 us (36%)
  loops' own time  134 us (18%)
  matrix products  122 us (17%)
  waiting for transfers between devices  68.1 us (9%)
  starting transfers between devices  64.5 us (9%)
  other arithmetic  50 us (7%)
  between operations  15.6 us (2%)
    another operation x1, loops' own time, body(): lax.fori_loop(0, slot_count, add_one, jnp.zeros((2, TS, TS), jnp.float32))  134 us
    gather x96, local copies, waits for them, and re-layouts  86.1 us
    dynamic_slice x64, local copies, waits for them, and re-layouts, add_one(): corner = (zero_index, rows_at[slot_at], cols_at[slot_at])  85.3 us
    ppermute x24, starting transfers between devices, shifted(): lax.ppermute(value, axis, [(source, source + steps) for source in range(l...  64.4 us
    dynamic_update_slice x64, local copies, waits for them, and re-layouts, add_one(): return lax.dynamic_update_slice(partial_value, window + subgrid, corner)  51.6 us
    psum x1, waiting for transfers between devices, body(): model_grid = lax.psum(tile_sum, 'af') * taper[None]  38.2 us
    dot_general x1, matrix products, grid_blocks(): first = jnp.einsum('krl,krc->klc', cos_u, weighted, precision=highest)  34.2 us
    ppermute x24, waiting for transfers between devices, shifted(): lax.ppermute(value, axis, [(source, source + steps) for source in range(l...  29.2 us
  transfers between devices with their start and end apart: 26, of which 13 were waited for; matrix products, arithmetic and copies ran while one was open for 11% of the time, Pallas kernels for 0%

commit v1 on v0

v1 whole, which is shorter than its diff:
```python
import math

import jax
import jax.numpy as jnp
import numpy as np
from jax import lax
from jax.experimental import pallas as pl
from jax.experimental.pallas import tpu as pltpu
from jax.sharding import PartitionSpec as P

S = 64
CAP = 2
NB = 16
TS = 512
BF = jnp.bfloat16
F32 = jnp.float32
MESH = pl.DeviceIdType.MESH
ROUTES = tuple((r, c) for r in (-1, 0, 1) for c in (-1, 0, 1) if (r, c) != (0, 0))
NR = len(ROUTES)
NSLOT = NR * CAP + NB
VMEM_LIMIT = 56 * 1024 * 1024


def fit(fn, count):
    k = np.arange(400)
    z = 0.125 * (1.0 + np.cos(np.pi * (k + 0.5) / 400))
    cheb = np.polynomial.chebyshev.Chebyshev.fit(z, fn(np.sqrt(z)), count - 1, domain=[0, 0.25])
    return [float(v) for v in cheb.convert(kind=np.polynomial.Polynomial).coef]


COS = fit(lambda t: np.cos(2 * np.pi * t), 8)
SIN = fit(lambda t: np.sin(2 * np.pi * t) / t, 8)


def dft_tables():
    pos = np.arange(S)
    ang = (pos[:, None] * pos[None, :] % S) * (2.0 * np.pi / S)
    return np.cos(ang) / math.sqrt(S), -np.sin(ang) / math.sqrt(S)


def split_np(x):
    x = x.astype(np.float32)
    hi = x.astype(BF).astype(np.float32)
    return hi, (x - hi).astype(BF).astype(np.float32)


def constants():
    fr, fi = dft_tables()
    hi, lo = split_np(np.concatenate([fr, fi], 0))
    left = np.concatenate([hi, hi, lo, lo], 1)
    out = [left]
    for sign in (1, -1):
        right = np.concatenate(
            [np.concatenate([fr, sign * fi], 1), np.concatenate([-sign * fi, fr], 1)], 0
        )
        hi, lo = split_np(right)
        out.append(np.concatenate([np.concatenate([hi, hi], 0), np.concatenate([lo, lo], 0)], 1))
    return [v.astype(BF) for v in out]


def split(x):
    hi = x.astype(BF)
    return hi, (x - hi.astype(F32)).astype(BF)


def horner(coefs, z):
    acc = jnp.full(z.shape, coefs[-1], F32)
    for c in coefs[-2::-1]:
        acc = acc * z + c
    return acc


def cos_sin(turns):
    t = turns - jnp.round(turns)
    z = t * t
    return horner(COS, z), horner(SIN, z) * t


def phases(u):
    j = lax.broadcasted_iota(jnp.int32, (8, u.shape[1]), 0).astype(F32)
    c1, s1 = cos_sin(u * (j * (1.0 / 64)))
    c2, s2 = cos_sin(u * (j * 0.125 - 0.5))
    cs, ss = [], []
    for k in range(8):
        ck, sk = c2[k : k + 1], s2[k : k + 1]
        cs.append(ck * c1 - sk * s1)
        ss.append(sk * c1 + ck * s1)
    return jnp.concatenate(cs, 0), jnp.concatenate(ss, 0)


def low_half(shape):
    return lax.broadcasted_iota(jnp.int32, shape, 1) < S


def rotate(x):
    y = pltpu.roll(x, S, 1)
    return jnp.where(low_half(x.shape), -y, y)


def times(x, a, conj):
    low = low_half(x.shape)
    ra = pltpu.roll(a, S, 1)
    rr = jnp.where(low, a, ra)
    ii = jnp.where(low, ra, a)
    y = pltpu.roll(x, S, 1) * ii
    sgn = low if conj else jnp.logical_not(low)
    return x * rr + jnp.where(sgn, y, -y)


def dft2(x, left, right, conj):
    hi, lo = split(x)
    m = jnp.dot(left, jnp.concatenate([hi, lo, hi, lo], 0), preferred_element_type=F32)
    turned = rotate(m[S:])
    y = m[:S] - turned if conj else m[:S] + turned
    hi, lo = split(y)
    m = jnp.dot(jnp.concatenate([hi, lo], 1), right, preferred_element_type=F32)
    return m[:, : 2 * S] + m[:, 2 * S :]


def image_kernel(vis_ref, coord_ref, out_ref):
    rows = vis_ref.shape[1] // 2

    def step(b, _):
        at = pl.ds(b, 1)
        cu, su = phases(coord_ref[at, :rows])
        cv, sv = phases(coord_ref[at, rows:])
        vr, vi = vis_ref[at, :rows], vis_ref[at, rows:]
        ahi, alo = split(jnp.concatenate([cu, su], 0))
        bhi, blo = split(jnp.concatenate([vr * cv - vi * sv, vr * sv + vi * cv], 0))
        m = lax.dot_general(
            jnp.concatenate([ahi, alo], 0),
            jnp.concatenate([bhi, blo], 0),
            (((1,), (1,)), ((), ())),
            preferred_element_type=F32,
        )
        m = m[: 2 * S] + m[2 * S :]
        m = m[:, : 2 * S] + m[:, 2 * S :]
        out_ref[b] = (m[:S] + rotate(m[S:])) * (1.0 / math.sqrt(rows))
        return 0

    lax.fori_loop(0, NB, step, 0)


def subgrid_kernel(n_vert, per_dev, cap, me_ref, info_ref, image_ref, beam_ref, left_ref, right_ref,
                   out_ref, aterm_ref, where_ref, count_ref, heads_ref):
    me = me_ref[0]
    n = info_ref.shape[0]
    row, col = me // n_vert, me % n_vert

    def zero(i, _):
        count_ref[i] = 0
        return 0

    lax.fori_loop(0, n, zero, 0)
    for i in range(9):
        heads_ref[i] = 0
    live = info_ref[me, 5 * NB]

    def find(station):
        keeper = station // per_dev
        order = count_ref[keeper]
        count_ref[keeper] = order + 1
        return lax.rem(me - keeper + n, n) * cap + order

    def step(b, _):
        first = find(info_ref[me, 3 * NB + b])
        second = find(info_ref[me, 4 * NB + b])
        owner = info_ref[me, b]
        head = (owner // n_vert - row + 1) * 3 + (owner % n_vert - col + 1)
        head = jnp.where(b < live, head, 4)
        order = heads_ref[head]
        heads_ref[head] = order + 1
        slot = jnp.where(head == 4, NR * CAP + b, jnp.where(head < 4, head, head - 1) * CAP + order)
        where_ref[b] = slot
        p = beam_ref[first].astype(F32)
        q = beam_ref[second].astype(F32)
        aterm = times(p, q, True)
        aterm_ref[b] = aterm
        out_ref[slot] = dft2(times(image_ref[b], aterm, False), left_ref[...], right_ref[...], False)
        return 0

    lax.fori_loop(0, NB, step, 0)


def incoming(n_vert, n_au, me, info_ref, visit):
    row, col = me // n_vert, me % n_vert
    for route, (dr, dc) in enumerate(ROUTES):
        sr, sc = row - dr, col - dc
        inside = (sr >= 0) & (sr < n_au) & (sc >= 0) & (sc < n_vert)

        @pl.when(inside)
        def _(route=route, src=sr * n_vert + sc):
            live = info_ref[src, 5 * NB]

            def look(b, count):
                hit = info_ref[src, b] == me

                @pl.when(hit)
                def _():
                    visit(route * CAP + count, info_ref[src, NB + b], info_ref[src, 2 * NB + b])

                return count + hit.astype(jnp.int32)

            lax.fori_loop(0, live, look, jnp.int32(0))

    def own(b, _):
        @pl.when(info_ref[me, b] == me)
        def _():
            visit(NR * CAP + b, info_ref[me, NB + b], info_ref[me, 2 * NB + b])

        return 0

    lax.fori_loop(0, info_ref[me, 5 * NB], own, 0)


def tile_kernel(n_vert, n_au, me_ref, info_ref, got_ref, mine_ref, out_ref, pad_ref):
    pad_ref[...] = jnp.zeros_like(pad_ref)
    low = low_half((S, 2 * S))
    blank = jnp.zeros((S, 2 * S), F32)
    blank_rows = jnp.zeros((8, 256), F32)

    def visit(slot, row_at, col_at):
        top = pl.multiple_of(row_at // 8 * 8, 8)
        start = pl.multiple_of(col_at // 128 * 128, 128)
        shift = col_at % 128

        def put(x):
            for plane in range(2):
                part = x if plane == 0 else pltpu.roll(x, S, 1)
                wide = jnp.concatenate([jnp.where(low, part, 0.0), blank], 1)
                wide = jnp.concatenate([pltpu.roll(wide, shift, 1), blank_rows], 0)
                at = (plane, pl.ds(top, S + 8), pl.ds(start, 256))
                pad_ref[at] += pltpu.roll(wide, row_at % 8, 0)

        @pl.when(slot < NR * CAP)
        def _():
            put(got_ref[jnp.minimum(slot, NR * CAP - 1)])

        @pl.when(slot >= NR * CAP)
        def _():
            put(mine_ref[slot])

    incoming(n_vert, n_au, me_ref[0], info_ref, visit)
    out_ref[...] = pad_ref[:, :TS, :TS]


def window_kernel(n_vert, n_au, me_ref, info_ref, tile_ref, other_ref, taper_ref, model_ref, win_ref, pad_ref):
    total = tile_ref[...]
    for k in range(other_ref.shape[0]):
        total = total + other_ref[k]
    model = total * taper_ref[...][None]
    model_ref[...] = model
    pad_ref[:, :TS, :TS] = model
    pad_ref[:, :TS, TS:] = jnp.zeros((2, TS, 128), F32)
    pad_ref[:, TS:, :] = jnp.zeros((2, 8, TS + 128), F32)
    low = low_half((S, 2 * S))

    def visit(slot, row_at, col_at):
        top = pl.multiple_of(row_at // 8 * 8, 8)
        lift = lax.rem(S + 8 - row_at % 8, S + 8)
        start = pl.multiple_of(col_at // 128 * 128, 128)
        shift = lax.rem(256 - col_at % 128, 256)
        parts = []
        for plane in range(2):
            wide = pad_ref[plane, pl.ds(top, S + 8), pl.ds(start, 256)]
            wide = pltpu.roll(wide, shift, 1)[:, : 2 * S]
            parts.append(pltpu.roll(wide, lift, 0)[:S])
        win_ref[slot] = jnp.where(low, parts[0], pltpu.roll(parts[1], S, 1))

    incoming(n_vert, n_au, me_ref[0], info_ref, visit)


def degrid_kernel(me_ref, info_ref, where_ref, got_ref, mine_ref, aterm_ref, coord_ref, left_ref, right_ref,
                  out_ref, win_ref):
    rows = coord_ref.shape[1] // 2
    live = info_ref[me_ref[0], 5 * NB]
    out_ref[...] = jnp.zeros_like(out_ref)

    def step(b, _):
        slot = where_ref[b]

        @pl.when(slot < NR * CAP)
        def _():
            win_ref[...] = got_ref[jnp.minimum(slot, NR * CAP - 1)]

        @pl.when(slot >= NR * CAP)
        def _():
            win_ref[...] = mine_ref[slot]

        back = times(dft2(win_ref[...], left_ref[...], right_ref[...], True), aterm_ref[b], True)
        hi = back.astype(BF).astype(F32)
        both = jnp.concatenate([hi, back - hi], 0).T.astype(BF)
        at = pl.ds(b, 1)
        cu, su = phases(coord_ref[at, :rows])
        cv, sv = phases(coord_ref[at, rows:])
        ehi, elo = split(jnp.concatenate([cu, su], 1))
        m = jnp.dot(
            jnp.concatenate([both, both], 1),
            jnp.concatenate([ehi, ehi, elo, elo], 0),
            preferred_element_type=F32,
        )
        a_real = m[:S, :rows] + m[S:, rows:]
        a_imag = m[S:, :rows] - m[:S, rows:]
        real = jnp.sum(a_real * cv + a_imag * sv, axis=0, keepdims=True)
        imag = jnp.sum(a_imag * cv - a_real * sv, axis=0, keepdims=True)
        out_ref[at, :] = jnp.concatenate([real, imag], 1) * (1.0 / S)
        return 0

    lax.fori_loop(0, live, step, 0)


def beam_exchange_kernel(n_vert, cap, ids_ref, beam_ref, out_ref, send_ref, send_sem, recv_sem, own_sem):
    n = out_ref.shape[0]
    me = lax.axis_index("au") * n_vert + lax.axis_index("vert")
    barrier = pltpu.get_barrier_semaphore()

    def peer(k):
        t = lax.rem(me + k, n)
        return {"au": t // n_vert, "vert": t % n_vert}

    for k in range(1, n):
        pl.semaphore_signal(barrier, inc=1, device_id=peer(k), device_id_type=MESH)

    def fill(k, _):
        for j in range(cap):
            send_ref[k, j * S : (j + 1) * S, :] = beam_ref[ids_ref[k * cap + j]]
        return 0

    lax.fori_loop(0, n, fill, 0)
    own = pltpu.make_async_copy(send_ref.at[0], out_ref.at[0], own_sem)
    own.start()
    pl.semaphore_wait(barrier, n - 1)
    copies = []
    for k in range(1, n):
        copies.append(pltpu.make_async_remote_copy(
            send_ref.at[k], out_ref.at[k], send_sem.at[k], recv_sem.at[k],
            device_id=peer(k), device_id_type=MESH))
        copies[-1].start()
    own.wait()
    for copy in copies:
        copy.wait()


def route_kernel(n_au, n_vert, sign, in_ref, out_ref, send_sem, recv_sem):
    row, col = lax.axis_index("au"), lax.axis_index("vert")
    barrier = pltpu.get_barrier_semaphore()

    def inside(dr, dc):
        return (row + dr >= 0) & (row + dr < n_au) & (col + dc >= 0) & (col + dc < n_vert)

    for dr, dc in ROUTES:
        @pl.when(inside(dr, dc))
        def _():
            pl.semaphore_signal(barrier, inc=1, device_id={"au": row + dr, "vert": col + dc},
                                device_id_type=MESH)
    tall = 1 + jnp.minimum(row, 1) + jnp.minimum(n_au - 1 - row, 1)
    wide = 1 + jnp.minimum(col, 1) + jnp.minimum(n_vert - 1 - col, 1)
    pl.semaphore_wait(barrier, tall * wide - 1)

    def copy_of(i, dr, dc):
        at = pl.ds(i * CAP, CAP)
        return pltpu.make_async_remote_copy(
            in_ref.at[at], out_ref.at[at], send_sem.at[i], recv_sem.at[i],
            device_id={"au": row + dr, "vert": col + dc}, device_id_type=MESH)

    for i, (dr, dc) in enumerate(ROUTES):
        dr, dc = sign * dr, sign * dc

        @pl.when(inside(dr, dc))
        def _():
            copy_of(i, dr, dc).start()
    for i, (dr, dc) in enumerate(ROUTES):
        dr, dc = sign * dr, sign * dc

        @pl.when(inside(dr, dc))
        def _():
            copy_of(i, dr, dc).wait_send()

        @pl.when(inside(-dr, -dc))
        def _():
            copy_of(i, dr, dc).wait_recv()


def tile_exchange_kernel(in_ref, out_ref, send_sem, recv_sem):
    n = out_ref.shape[0] + 1
    me = lax.axis_index("af")
    barrier = pltpu.get_barrier_semaphore()
    for k in range(1, n):
        pl.semaphore_signal(barrier, inc=1, device_id={"af": lax.rem(me + k, n)}, device_id_type=MESH)
    pl.semaphore_wait(barrier, n - 1)
    copies = []
    for k in range(1, n):
        copies.append(pltpu.make_async_remote_copy(
            in_ref, out_ref.at[k - 1], send_sem.at[k - 1], recv_sem.at[k - 1],
            device_id={"af": lax.rem(me + k, n)}, device_id_type=MESH))
        copies[-1].start()
    for copy in copies:
        copy.wait()


SMEM = pl.BlockSpec(memory_space=pltpu.SMEM)
VMEM = pl.BlockSpec(memory_space=pltpu.VMEM)
ANY = pl.BlockSpec(memory_space=pl.ANY)


def shape(*dims, dtype=F32):
    return jax.ShapeDtypeStruct(dims, dtype)


def local_call(kernel, in_specs, out_specs, out_shape, scratch=()):
    return pl.pallas_call(
        kernel, in_specs=in_specs, out_specs=out_specs, out_shape=out_shape,
        scratch_shapes=list(scratch),
        compiler_params=pltpu.CompilerParams(vmem_limit_bytes=VMEM_LIMIT))


def remote_call(kernel, ident, in_specs, out_shape, scratch):
    return pl.pallas_call(
        kernel, in_specs=in_specs, out_specs=ANY, out_shape=out_shape, scratch_shapes=scratch,
        compiler_params=pltpu.CompilerParams(
            collective_id=ident, has_side_effects=True, vmem_limit_bytes=VMEM_LIMIT))


def body(visib, coords, owner, offsets, stations, live, beams, taper):
    n_au, n_vert, n_af = lax.axis_size("au"), lax.axis_size("vert"), lax.axis_size("af")
    n = n_au * n_vert
    per_dev = beams.shape[1]
    cap = 2 * NB // n + 2
    me = lax.axis_index("au") * n_vert + lax.axis_index("vert")
    mine = me.astype(jnp.int32).reshape(1)
    signal, places = visib[0], coords[0]
    rows2 = signal.shape[1]
    info = jnp.concatenate(
        [owner[0], offsets[0, :, 0], offsets[0, :, 1], stations[0, :, 0], stations[0, :, 1],
         jnp.broadcast_to(live[0, 0], (128 - 5 * NB,))])
    info = lax.all_gather(info, ("au", "vert"), axis=0)
    left, right, right_conj = constants()

    images = local_call(image_kernel, [VMEM] * 2, VMEM, shape(NB, S, 2 * S))(signal, places)

    asked = jnp.roll(info[:, 3 * NB : 5 * NB], -me, axis=0).reshape(n, 2, NB)
    asked = asked.transpose(0, 2, 1).reshape(n, 2 * NB)
    hit = asked // per_dev == me
    entry = jnp.arange(2 * NB, dtype=jnp.int32)
    order = jnp.sum((hit[:, None, :] & (entry[None, :] < entry[:, None])[None]).astype(jnp.int32), axis=2)
    pick = hit[:, None, :] & (order[:, None, :] == jnp.arange(cap, dtype=jnp.int32)[None, :, None])
    ids = jnp.sum(jnp.where(pick, (asked % per_dev)[:, None, :], 0), axis=2).reshape(n * cap)
    found = remote_call(
        lambda *refs: beam_exchange_kernel(n_vert, cap, *refs), 1, [SMEM, VMEM],
        shape(n, cap * S, 2 * S, dtype=BF),
        [pltpu.VMEM((n, cap * S, 2 * S), BF), pltpu.SemaphoreType.DMA((n,)),
         pltpu.SemaphoreType.DMA((n,)), pltpu.SemaphoreType.DMA],
    )(ids, beams[0].reshape(per_dev, S, 2 * S))

    subgrids, aterms, slots = local_call(
        lambda *refs: subgrid_kernel(n_vert, per_dev, cap, *refs),
        [SMEM, SMEM] + [VMEM] * 4, [VMEM, VMEM, SMEM],
        [shape(NSLOT, S, 2 * S), shape(NB, S, 2 * S), shape(NB, dtype=jnp.int32)],
        [pltpu.SMEM((n,), jnp.int32), pltpu.SMEM((9,), jnp.int32)],
    )(mine, info, images, found.reshape(n * cap, S, 2 * S), left, right)

    def routed(values, sign, ident):
        return remote_call(
            lambda *refs: route_kernel(n_au, n_vert, sign, *refs), ident, [ANY],
            shape(NR * CAP, S, 2 * S),
            [pltpu.SemaphoreType.DMA((NR,)), pltpu.SemaphoreType.DMA((NR,))])(values)

    arrived = routed(subgrids, 1, 2)
    tile = local_call(
        lambda *refs: tile_kernel(n_vert, n_au, *refs), [SMEM, SMEM, VMEM, VMEM], VMEM,
        shape(2, TS, TS), [pltpu.VMEM((2, TS + 8, TS + 128), F32)])(mine, info, arrived, subgrids)
    others = remote_call(
        tile_exchange_kernel, 3, [ANY], shape(n_af - 1, 2, TS, TS),
        [pltpu.SemaphoreType.DMA((n_af - 1,)), pltpu.SemaphoreType.DMA((n_af - 1,))])(tile)
    model_grid, windows = local_call(
        lambda *refs: window_kernel(n_vert, n_au, *refs), [SMEM, SMEM] + [VMEM] * 3, [VMEM, VMEM],
        [shape(2, TS, TS), shape(NSLOT, S, 2 * S)], [pltpu.VMEM((2, TS + 8, TS + 128), F32)],
    )(mine, info, tile, others, taper)
    returned = routed(windows, -1, 4)
    result = local_call(
        degrid_kernel, [SMEM] * 3 + [VMEM] * 6, VMEM, shape(NB, rows2), [pltpu.VMEM((S, 2 * S), F32)],
    )(mine, info, slots, returned, windows, aterms, places, left, right_conj)
    return (result[None], model_grid)


def solution(mesh):
    placed = (
        P("af", ("au", "vert"), None),
        P("af", ("au", "vert"), None),
        P("af", ("au", "vert")),
        P("af", ("au", "vert"), None),
        P("af", ("au", "vert"), None),
        P("af", ("au", "vert")),
        P("af", ("au", "vert"), None),
        P("au", "vert"),
    )
    return jax.shard_map(
        body,
        mesh=mesh,
        in_specs=placed,
        out_specs=(P("af", ("au", "vert"), None), P(None, "au", "vert")),
        check_vma=False,
    )
```

time: 737 us -> 147 us (0.20); the launches traced: 722 us -> 146 us
  local copies, waits for them, and re-layouts: 268 us -> 4.46 us
  loops' own time: 134 us -> 0 us
  matrix products: 122 us -> 0 us
  Pallas kernels: 0 us -> 111 us
  waiting for transfers between devices: 68.1 us -> 0 us
  starting transfers between devices: 64.5 us -> 0 us
  other arithmetic: 50 us -> 0.54 us
  blocking collectives: 0 us -> 28.8 us
  between operations: 15.6 us -> 1.39 us
    another operation x2 -> x0, loops' own time: 134 us -> none  [the longest x1 134 us: body(): lax.fori_loop(0, slot_count, add_one, jnp.zeros((2, TS, TS), jnp.float32))]
    dot_general x11 -> x0, matrix products: 122 us -> none  [the longest x1 34.2 us: grid_blocks(): first = jnp.einsum('krl,krc->klc', cos_u, weighted, precision=highest)]
    dynamic_slice x128 -> x0, local copies, waits for them, and re-layouts: 113 us -> none  [the longest x64 85.3 us: add_one(): corner = (zero_index, rows_at[slot_at], cols_at[slot_at])]
    pallas_call x0 -> x9, Pallas kernels: none -> 111 us  [the longest x1 27.9 us: body(): remote_call(lambda *refs: beam_exchange_kernel(n_vert, cap, *refs), 1, [S...]
    gather x101 -> x0, local copies, waits for them, and re-layouts: 88 us -> none
    ppermute x24 -> x0, starting transfers between devices: 64.4 us -> none  [shifted(): lax.ppermute(value, axis, [(source, source + steps) for source in range(l...]
    dynamic_update_slice x64 -> x0, local copies, waits for them, and re-layouts: 51.6 us -> none  [add_one(): return lax.dynamic_update_slice(partial_value, window + subgrid, corner)]
    psum x1 -> x0, waiting for transfers between devices: 38.2 us -> none  [body(): model_grid = lax.psum(tile_sum, 'af') * taper[None]]
  transfers between devices with their start and end apart: 26 -> 0, of which waited for: 13 -> 0; matrix products, arithmetic and copies ran while one was open for 11% -> 0% of each run, Pallas kernels for 0% -> 0%
where the time goes in v1:
time: 147 us; the launch traced here: 146 us
  Pallas kernels  111 us (76%)
  blocking collectives  28.8 us (20%)
  local copies, waits for them, and re-layouts  4.46 us (3%)
    all_gather x1, blocking collectives, body(): info = lax.all_gather(info, ('au', 'vert'), axis=0)  28.8 us
    pallas_call x1, Pallas kernels, body(): remote_call(lambda *refs: beam_exchange_kernel(n_vert, cap, *refs), 1, [S...  27.9 us
    pallas_call x2, Pallas kernels, routed(): remote_call(lambda *refs: route_kernel(n_au, n_vert, sign, *refs), ident,...  24.6 us
    pallas_call x1, Pallas kernels, body(): local_call(degrid_kernel, [SMEM] * 3 + [VMEM] * 6, VMEM, shape(NB, rows2)...  14.1 us
    pallas_call x1, Pallas kernels, body(): local_call(lambda *refs: subgrid_kernel(n_vert, per_dev, cap, *refs), [SM...  10.9 us
    pallas_call x1, Pallas kernels, body(): local_call(image_kernel, [VMEM] * 2, VMEM, shape(NB, S, 2 * S))  9.25 us
    pallas_call x1, Pallas kernels, body(): local_call(lambda *refs: window_kernel(n_vert, n_au, *refs), [SMEM, SMEM]...  8.57 us
    pallas_call x1, Pallas kernels, body(): remote_call(tile_exchange_kernel, 3, [ANY], shape(n_af - 1, 2, TS, TS), [...  8.17 us

profile of v1, /device:TPU:9, one launch (start us, length us, event | category | flops | bytes accessed | tf_op | source)
XLA Modules:
  0.0 146.3 jit_solution(3926293386719819741)
XLA Ops:
  1.3 0.8 slice_bitcast_fusion
  2.1 0.7 concatenate.7
  2.8 28.8 %all-gather.1 = s32[16,1,128]{2,1,0:T(1,128)S(1)} all-gather(s32[1,1,128]{2,1,0:T(1,128)S(1)} %bitcast.37), channel_id=2, replica_groups=mesh['au'=4,'vert'=4,'af'=2] {'au','vert'}, dimensions={0}, use_global_device_ids=true | all-gather | bytes 8704 | tf_op jit(solution)/shard_map/all_gather | solution.py:436
  31.6 0.0 copy-start
  31.6 0.1 slice.20
  31.7 0.1 reshape.83
  31.8 0.1 copy.32
  31.9 0.1 copy.33
  32.0 0.3 convert_reduce_fusion
  32.3 0.1 select_reduce_fusion
  32.5 0.1 copy.37
  32.6 0.6 reshape.85.refs_0_
  33.2 9.3 %shard_map.122.refs_2_ = f32[16,64,128]{2,1,0:T(8,128)} custom-call(f32[16,1024]{1,0:T(8,128)} %bitcast.33, f32[16,1024]{1,0:T(8,128)} %bitcast.31), custom_call_target="tpu_custom_call" | custom-call | tf_op jit(solution)/shard_map/pallas_call | solution.py:439
  42.4 2.0 %copy.38 = bf16[4,8,64,128]{3,2,1,0:T(8,128)(2,1)} copy(bf16[4,8,64,128]{3,1,2,0:T(8,128)(2,1)} %bitcast.25) | data formatting | bytes 1048576
  44.4 27.9 %shard_map.123 = bf16[16,256,128]{2,1,0:T(8,128)(2,1)} custom-call(s32[64]{0:T(128)} %reshape.85.refs_0_, bf16[32,64,128]{2,1,0:T(8,128)(2,1)} %bitcast.24), custom_call_target="tpu_custom_call" | custom-call | tf_op jit(solution)/shard_map/pallas_call | solution.py:448
  72.3 0.0 copy-done
  72.3 10.9 %shard_map.124 = (f32[32,64,128]{2,1,0:T(8,128)}, f32[16,64,128]{2,1,0:T(8,128)}, s32[16]{0:T(128)}) custom-call(s32[1]{0:T(128)} %bitcast.refs_0_.me_ref, s32[16,128]{1,0:T(8,128)} %bitcast.27, f32[16,64,128]{2,1,0:T(8,128)} %shard_map.122.refs_2_, bf16[64,64,128]{2,1,0:T(8,128)(2,1)} %bitcast.23, bf16[128,256]{1,0:T(8,128)(2,1)} %constant.67.clone.refs_4_.left_ref, ...), custom_call_target="tpu_custom_call" | custom-call | tf_op jit(solution)/shard_map/pallas_call | solution.py:455
  83.2 7.5 %shard_map.125.refs_2_ = f32[16,64,128]{2,1,0:T(8,128)} custom-call(f32[32,64,128]{2,1,0:T(8,128)} %get-tuple-element.8.refs_0_.refs_3_), custom_call_target="tpu_custom_call" | custom-call | tf_op jit(solution)/shard_map/pallas_call | solution.py:463
  90.6 7.7 %shard_map.126.in_ref.refs_2_ = f32[2,512,512]{2,1,0:T(8,128)} custom-call(s32[1]{0:T(128)} %bitcast.refs_0_.me_ref, s32[16,128]{1,0:T(8,128)} %bitcast.28, f32[16,64,128]{2,1,0:T(8,128)} %shard_map.125.refs_2_, f32[32,64,128]{2,1,0:T(8,128)} %get-tuple-element.8.refs_0_.refs_3_), custom_call_target="tpu_custom_call" | custom-call | tf_op jit(solution)/shard_map/pallas_call | solution.py:469
  98.3 8.2 %shard_map.127.refs_3_ = f32[1,2,512,512]{3,2,1,0:T(8,128)} custom-call(f32[2,512,512]{2,1,0:T(8,128)} %shard_map.126.in_ref.refs_2_), custom_call_target="tpu_custom_call" | custom-call | tf_op jit(solution)/shard_map/pallas_call | solution.py:472
  106.5 8.6 %shard_map.128 = (f32[2,512,512]{2,1,0:T(8,128)}, f32[32,64,128]{2,1,0:T(8,128)}) custom-call(s32[1]{0:T(128)} %bitcast.refs_0_.me_ref, s32[16,128]{1,0:T(8,128)} %bitcast.29, f32[2,512,512]{2,1,0:T(8,128)} %shard_map.126.in_ref.refs_2_, f32[1,2,512,512]{3,2,1,0:T(8,128)} %shard_map.127.refs_3_, f32[512,512]{1,0:T(8,128)} %refs_4_.2), custom_call_target="tpu_custom_call" | custom-call | tf_op jit(solution)/shard_map/pallas_call | solution.py:475
  115.0 17.1 %shard_map.129.got_ref = f32[16,64,128]{2,1,0:T(8,128)} custom-call(f32[32,64,128]{2,1,0:T(8,128)} %get-tuple-element.9.refs_0_.mine_ref), custom_call_target="tpu_custom_call" | custom-call | tf_op jit(solution)/shard_map/pallas_call | solution.py:463
  132.2 14.1 %shard_map.130 = f32[16,1024]{1,0:T(8,128)} custom-call(s32[1]{0:T(128)} %bitcast.refs_0_.me_ref, s32[16,128]{1,0:T(8,128)} %bitcast.30, s32[16]{0:T(128)} %get-tuple-element.7.where_ref, f32[16,64,128]{2,1,0:T(8,128)} %shard_map.129.got_ref, f32[32,64,128]{2,1,0:T(8,128)} %get-tuple-element.9.refs_0_.mine_ref, f32[16,64,128]{2,1,0:T(8,128)} %get-tuple-element.10.aterm_ref, ...), custom_call_target="tpu_custom_call" | custom-call | tf_op jit(solution)/shard_map/pallas_call | solution.py:480
  (5 shorter events, 0.1 us)
Async XLA Ops:
  31.6 40.7 %copy-start = (s32[16,1,128]{2,1,0:T(1,128)}, s32[16,1,128]{2,1,0:T(1,128)S(1)}, u32[]{:S(2)}) copy-start(s32[16,1,128]{2,1,0:T(1,128)S(1)} %all-gather.1) | copy-start | bytes 24580

commit v2 on v1

--- a/solution.py
+++ b/solution.py
@@ -18,7 +18,7 @@
 ROUTES = tuple((r, c) for r in (-1, 0, 1) for c in (-1, 0, 1) if (r, c) != (0, 0))
 NR = len(ROUTES)
 NSLOT = NR * CAP + NB
-VMEM_LIMIT = 56 * 1024 * 1024
+VMEM_LIMIT = 32 * 1024 * 1024
 
 
 def fit(fn, count):
@@ -107,17 +107,22 @@
     return x * rr + jnp.where(sgn, y, -y)
 
 
-def dft2(x, left, right, conj):
-    hi, lo = split(x)
+def dft2(blocks, left, right, conj):
+    width = 2 * S
+    hi, lo = split(jnp.concatenate(blocks, 1) if len(blocks) > 1 else blocks[0])
     m = jnp.dot(left, jnp.concatenate([hi, lo, hi, lo], 0), preferred_element_type=F32)
-    turned = rotate(m[S:])
-    y = m[:S] - turned if conj else m[:S] + turned
-    hi, lo = split(y)
+    rows = []
+    for i in range(len(blocks)):
+        part = m[:, i * width : (i + 1) * width]
+        turned = rotate(part[S:])
+        rows.append(part[:S] - turned if conj else part[:S] + turned)
+    hi, lo = split(jnp.concatenate(rows, 0))
     m = jnp.dot(jnp.concatenate([hi, lo], 1), right, preferred_element_type=F32)
-    return m[:, : 2 * S] + m[:, 2 * S :]
-
-
-def image_kernel(vis_ref, coord_ref, out_ref):
+    m = m[:, :width] + m[:, width:]
+    return [m[i * S : (i + 1) * S] for i in range(len(blocks))]
+
+
+def make_images(vis_ref, coord_ref, out_ref):
     rows = vis_ref.shape[1] // 2
 
     def step(b, _):
@@ -162,7 +167,7 @@
         count_ref[keeper] = order + 1
         return lax.rem(me - keeper + n, n) * cap + order
 
-    def step(b, _):
+    def place(b):
         first = find(info_ref[me, 3 * NB + b])
         second = find(info_ref[me, 4 * NB + b])
         owner = info_ref[me, b]
@@ -172,14 +177,23 @@
         heads_ref[head] = order + 1
         slot = jnp.where(head == 4, NR * CAP + b, jnp.where(head < 4, head, head - 1) * CAP + order)
         where_ref[b] = slot
-        p = beam_ref[first].astype(F32)
-        q = beam_ref[second].astype(F32)
-        aterm = times(p, q, True)
-        aterm_ref[b] = aterm
-        out_ref[slot] = dft2(times(image_ref[b], aterm, False), left_ref[...], right_ref[...], False)
-        return 0
-
-    lax.fori_loop(0, NB, step, 0)
+        return first, second, slot
+
+    def step(i, _):
+        places = [place(i * 4 + j) for j in range(4)]
+        blocks = []
+        for j in range(4):
+            p = beam_ref[places[j][0]].astype(F32)
+            q = beam_ref[places[j][1]].astype(F32)
+            aterm = times(p, q, True)
+            aterm_ref[i * 4 + j] = aterm
+            blocks.append(times(image_ref[i * 4 + j], aterm, False))
+        blocks = dft2(blocks, left_ref[...], right_ref[...], False)
+        for j in range(4):
+            out_ref[places[j][2]] = blocks[j]
+        return 0
+
+    lax.fori_loop(0, NB // 4, step, 0)
 
 
 def incoming(n_vert, n_au, me, info_ref, visit):
@@ -274,20 +288,33 @@
                   out_ref, win_ref):
     rows = coord_ref.shape[1] // 2
     live = info_ref[me_ref[0], 5 * NB]
-    out_ref[...] = jnp.zeros_like(out_ref)
-
-    def step(b, _):
+
+    def fetch(b, _):
         slot = where_ref[b]
 
         @pl.when(slot < NR * CAP)
         def _():
-            win_ref[...] = got_ref[jnp.minimum(slot, NR * CAP - 1)]
+            win_ref[b] = got_ref[jnp.minimum(slot, NR * CAP - 1)]
 
         @pl.when(slot >= NR * CAP)
         def _():
-            win_ref[...] = mine_ref[slot]
-
-        back = times(dft2(win_ref[...], left_ref[...], right_ref[...], True), aterm_ref[b], True)
+            win_ref[b] = mine_ref[slot]
+
+        return 0
+
+    lax.fori_loop(0, NB, fetch, 0)
+
+    def transform(i, _):
+        blocks = [win_ref[i * 4 + j] for j in range(4)]
+        blocks = dft2(blocks, left_ref[...], right_ref[...], True)
+        for j in range(4):
+            win_ref[i * 4 + j] = times(blocks[j], aterm_ref[i * 4 + j], True)
+        return 0
+
+    lax.fori_loop(0, NB // 4, transform, 0)
+
+    def predict(b):
+        back = win_ref[b]
         hi = back.astype(BF).astype(F32)
         both = jnp.concatenate([hi, back - hi], 0).T.astype(BF)
         at = pl.ds(b, 1)
@@ -303,13 +330,44 @@
         a_imag = m[S:, :rows] - m[:S, rows:]
         real = jnp.sum(a_real * cv + a_imag * sv, axis=0, keepdims=True)
         imag = jnp.sum(a_imag * cv - a_real * sv, axis=0, keepdims=True)
-        out_ref[at, :] = jnp.concatenate([real, imag], 1) * (1.0 / S)
-        return 0
-
-    lax.fori_loop(0, live, step, 0)
-
-
-def beam_exchange_kernel(n_vert, cap, ids_ref, beam_ref, out_ref, send_ref, send_sem, recv_sem, own_sem):
+        return jnp.concatenate([real, imag], 1) * (1.0 / S)
+
+    def step(i, _):
+        found = [predict(i * 2 + j) for j in range(2)]
+        for j in range(2):
+            out_ref[pl.ds(i * 2 + j, 1), :] = jnp.where(i * 2 + j < live, found[j], 0.0)
+        return 0
+
+    lax.fori_loop(0, NB // 2, step, 0)
+
+
+def info_kernel(n_vert, in_ref, out_ref, send_sem, recv_sem, own_sem):
+    n = out_ref.shape[0]
+    me = lax.axis_index("au") * n_vert + lax.axis_index("vert")
+    barrier = pltpu.get_barrier_semaphore()
+
+    def peer(k):
+        t = lax.rem(me + k, n)
+        return {"au": t // n_vert, "vert": t % n_vert}
+
+    for k in range(1, n):
+        pl.semaphore_signal(barrier, inc=1, device_id=peer(k), device_id_type=MESH)
+    own = pltpu.make_async_copy(in_ref, out_ref.at[me], own_sem)
+    own.start()
+    pl.semaphore_wait(barrier, n - 1)
+    copies = []
+    for k in range(1, n):
+        copies.append(pltpu.make_async_remote_copy(
+            in_ref, out_ref.at[me], send_sem.at[k], recv_sem.at[k],
+            device_id=peer(k), device_id_type=MESH))
+        copies[-1].start()
+    own.wait()
+    for copy in copies:
+        copy.wait()
+
+
+def beam_exchange_kernel(n_vert, cap, ids_ref, beam_ref, vis_ref, coord_ref, out_ref, image_ref,
+                         send_ref, send_sem, recv_sem, own_sem):
     n = out_ref.shape[0]
     me = lax.axis_index("au") * n_vert + lax.axis_index("vert")
     barrier = pltpu.get_barrier_semaphore()
@@ -336,6 +394,7 @@
             send_ref.at[k], out_ref.at[k], send_sem.at[k], recv_sem.at[k],
             device_id=peer(k), device_id_type=MESH))
         copies[-1].start()
+    make_images(vis_ref, coord_ref, image_ref)
     own.wait()
     for copy in copies:
         copy.wait()
@@ -414,9 +473,9 @@
         compiler_params=pltpu.CompilerParams(vmem_limit_bytes=VMEM_LIMIT))
 
 
-def remote_call(kernel, ident, in_specs, out_shape, scratch):
+def remote_call(kernel, ident, in_specs, out_shape, scratch, out_specs=ANY):
     return pl.pallas_call(
-        kernel, in_specs=in_specs, out_specs=ANY, out_shape=out_shape, scratch_shapes=scratch,
+        kernel, in_specs=in_specs, out_specs=out_specs, out_shape=out_shape, scratch_shapes=scratch,
         compiler_params=pltpu.CompilerParams(
             collective_id=ident, has_side_effects=True, vmem_limit_bytes=VMEM_LIMIT))
 
@@ -433,10 +492,12 @@
     info = jnp.concatenate(
         [owner[0], offsets[0, :, 0], offsets[0, :, 1], stations[0, :, 0], stations[0, :, 1],
          jnp.broadcast_to(live[0, 0], (128 - 5 * NB,))])
-    info = lax.all_gather(info, ("au", "vert"), axis=0)
+    info = remote_call(
+        lambda *refs: info_kernel(n_vert, *refs), 5, [VMEM], shape(n, 1, 128, dtype=jnp.int32),
+        [pltpu.SemaphoreType.DMA((n,)), pltpu.SemaphoreType.DMA((n,)), pltpu.SemaphoreType.DMA],
+        out_specs=VMEM,
+    )(info.reshape(1, 128)).reshape(n, 128)
     left, right, right_conj = constants()
-
-    images = local_call(image_kernel, [VMEM] * 2, VMEM, shape(NB, S, 2 * S))(signal, places)
 
     asked = jnp.roll(info[:, 3 * NB : 5 * NB], -me, axis=0).reshape(n, 2, NB)
     asked = asked.transpose(0, 2, 1).reshape(n, 2 * NB)
@@ -445,12 +506,13 @@
     order = jnp.sum((hit[:, None, :] & (entry[None, :] < entry[:, None])[None]).astype(jnp.int32), axis=2)
     pick = hit[:, None, :] & (order[:, None, :] == jnp.arange(cap, dtype=jnp.int32)[None, :, None])
     ids = jnp.sum(jnp.where(pick, (asked % per_dev)[:, None, :], 0), axis=2).reshape(n * cap)
-    found = remote_call(
-        lambda *refs: beam_exchange_kernel(n_vert, cap, *refs), 1, [SMEM, VMEM],
-        shape(n, cap * S, 2 * S, dtype=BF),
+    found, images = remote_call(
+        lambda *refs: beam_exchange_kernel(n_vert, cap, *refs), 1, [SMEM] + [VMEM] * 3,
+        [shape(n, cap * S, 2 * S, dtype=BF), shape(NB, S, 2 * S)],
         [pltpu.VMEM((n, cap * S, 2 * S), BF), pltpu.SemaphoreType.DMA((n,)),
          pltpu.SemaphoreType.DMA((n,)), pltpu.SemaphoreType.DMA],
-    )(ids, beams[0].reshape(per_dev, S, 2 * S))
+        out_specs=[ANY, VMEM],
+    )(ids, beams[0].reshape(per_dev, S, 2 * S), signal, places)
 
     subgrids, aterms, slots = local_call(
         lambda *refs: subgrid_kernel(n_vert, per_dev, cap, *refs),
@@ -478,7 +540,7 @@
     )(mine, info, tile, others, taper)
     returned = routed(windows, -1, 4)
     result = local_call(
-        degrid_kernel, [SMEM] * 3 + [VMEM] * 6, VMEM, shape(NB, rows2), [pltpu.VMEM((S, 2 * S), F32)],
+        degrid_kernel, [SMEM] * 3 + [VMEM] * 6, VMEM, shape(NB, rows2), [pltpu.VMEM((NB, S, 2 * S), F32)],
     )(mine, info, slots, returned, windows, aterms, places, left, right_conj)
     return (result[None], model_grid)
 

time: 147 us -> 96.1 us (0.65)
  blocking collectives: 28.8 us -> 0 us
  Pallas kernels: 111 us -> 86.8 us
    all_gather x1 -> x0, blocking collectives: 28.8 us -> none  [body(): info = lax.all_gather(info, ('au', 'vert'), axis=0)]
    pallas_call x1, Pallas kernels: 10.9 us -> 3.73 us  [body(): local_call(lambda *refs: subgrid_kernel(n_vert, per_dev, cap, *refs), [SM...]
    pallas_call x1, Pallas kernels: 14.1 us -> 7.93 us  [body(): local_call(degrid_kernel, [SMEM] * 3 + [VMEM] * 6, VMEM, shape(NB, rows2)...]
    pallas_call x2, Pallas kernels: 24.6 us -> 20.1 us  [routed(): remote_call(lambda *refs: route_kernel(n_au, n_vert, sign, *refs), ident,...]
    pallas_call x1, Pallas kernels: 7.66 us -> 3.98 us  [body(): local_call(lambda *refs: tile_kernel(n_vert, n_au, *refs), [SMEM, SMEM, V...]
    pallas_call x1, Pallas kernels: 8.17 us -> 11.6 us  [body(): remote_call(tile_exchange_kernel, 3, [ANY], shape(n_af - 1, 2, TS, TS), [...]
    pallas_call x1, Pallas kernels: 8.57 us -> 5.12 us  [body(): local_call(lambda *refs: window_kernel(n_vert, n_au, *refs), [SMEM, SMEM]...]
    pallas_call x1, Pallas kernels: 9.25 us -> 6.89 us  [body(): remote_call(lambda *refs: info_kernel(n_vert, *refs), 5, [VMEM], shape(n,...]
where the time goes in v2:
time: 96.1 us; the launch traced here: 94.5 us
  Pallas kernels  86.8 us (90%)
  local copies, waits for them, and re-layouts  5.69 us (6%)
  between operations  1.53 us (2%)
    pallas_call x1, Pallas kernels, body(): remote_call(lambda *refs: beam_exchange_kernel(n_vert, cap, *refs), 1, [S...  27.3 us
    pallas_call x2, Pallas kernels, routed(): remote_call(lambda *refs: route_kernel(n_au, n_vert, sign, *refs), ident,...  20.1 us
    pallas_call x1, Pallas kernels, body(): remote_call(tile_exchange_kernel, 3, [ANY], shape(n_af - 1, 2, TS, TS), [...  11.6 us
    pallas_call x1, Pallas kernels, body(): local_call(degrid_kernel, [SMEM] * 3 + [VMEM] * 6, VMEM, shape(NB, rows2)...  7.93 us
    pallas_call x1, Pallas kernels, body(): remote_call(lambda *refs: info_kernel(n_vert, *refs), 5, [VMEM], shape(n,...  6.89 us
    pallas_call x1, Pallas kernels, body(): local_call(lambda *refs: window_kernel(n_vert, n_au, *refs), [SMEM, SMEM]...  5.12 us
    pallas_call x1, Pallas kernels, body(): local_call(lambda *refs: tile_kernel(n_vert, n_au, *refs), [SMEM, SMEM, V...  3.98 us
    pallas_call x1, Pallas kernels, body(): local_call(lambda *refs: subgrid_kernel(n_vert, per_dev, cap, *refs), [SM...  3.73 us

profile of v2, /device:TPU:9, one launch (start us, length us, event | category | flops | bytes accessed | tf_op | source)
XLA Modules:
  0.0 94.5 jit_solution(3759745311126594113)
XLA Ops:
  0.6 0.0 copy-start.6
  1.4 0.8 slice_bitcast_fusion
  2.1 0.7 concatenate.7
  2.9 6.9 %shard_map.122 = s32[16,1,128]{2,1,0:T(1,128)S(1)} custom-call(s32[1,128]{1,0:T(1,128)S(1)} %bitcast.33), custom_call_target="tpu_custom_call" | custom-call | tf_op jit(solution)/shard_map/pallas_call | solution.py:495
  9.8 0.1 slice.20
  9.9 0.1 reshape.91
  9.9 0.1 copy.25
  10.0 0.1 copy.26
  10.1 0.3 convert_reduce_fusion
  10.5 0.1 select_reduce_fusion
  10.6 0.1 copy.30
  10.7 0.1 reshape.93.refs_0_
  10.8 1.2 %copy.31 = bf16[4,8,64,128]{3,2,1,0:T(8,128)(2,1)S(1)} copy(bf16[4,8,64,128]{3,1,2,0:T(8,128)(2,1)} %bitcast.34) | data formatting | bytes 1048576
  12.0 0.0 copy-start.1
  12.0 0.8 copy-done.1
  12.8 0.0 copy-start.7
  12.8 0.8 copy-done.7
  13.7 27.3 %shard_map.123 = (bf16[16,256,128]{2,1,0:T(8,128)(2,1)S(1)}, f32[16,64,128]{2,1,0:T(8,128)S(1)}) custom-call(s32[64]{0:T(128)S(1)} %reshape.93.refs_0_, bf16[32,64,128]{2,1,0:T(8,128)(2,1)S(1)} %bitcast.23, f32[16,1024]{1,0:T(8,128)S(1)} %bitcast.32, f32[16,1024]{1,0:T(8,128)S(1)} %bitcast.30), custom_call_target="tpu_custom_call" | custom-call | tf_op jit(solution)/shard_map/pallas_call | solution.py:509
  41.0 0.0 copy-done.6
  41.0 0.0 copy-start.3
  41.0 0.8 copy-done.3
  41.9 3.7 %shard_map.124 = (f32[32,64,128]{2,1,0:T(8,128)S(1)}, f32[16,64,128]{2,1,0:T(8,128)S(1)}, s32[16]{0:T(128)S(1)}) custom-call(s32[1]{0:T(128)} %bitcast.refs_0_.me_ref, s32[16,128]{1,0:T(8,128)S(1)} %bitcast.26, f32[16,64,128]{2,1,0:T(8,128)S(1)} %get-tuple-element.9.refs_2_, bf16[64,64,128]{2,1,0:T(8,128)(2,1)S(1)} %bitcast.24, ...), custom_call_target="tpu_custom_call" | custom-call | tf_op jit(solution)/shard_map/pallas_call | solution.py:517
  45.6 5.2 %shard_map.125.refs_2_ = f32[16,64,128]{2,1,0:T(8,128)S(1)} custom-call(f32[32,64,128]{2,1,0:T(8,128)S(1)} %get-tuple-element.12.refs_0_.refs_3_), custom_call_target="tpu_custom_call" | custom-call | tf_op jit(solution)/shard_map/pallas_call | solution.py:525
  50.8 4.0 %shard_map.126.in_ref.refs_2_ = f32[2,512,512]{2,1,0:T(8,128)S(1)} custom-call(s32[1]{0:T(128)} %bitcast.refs_0_.me_ref, s32[16,128]{1,0:T(8,128)S(1)} %bitcast.27, f32[16,64,128]{2,1,0:T(8,128)S(1)} %shard_map.125.refs_2_, f32[32,64,128]{2,1,0:T(8,128)S(1)} %get-tuple-element.12.refs_0_.refs_3_), custom_call_target="tpu_custom_call" | custom-call | tf_op jit(solution)/shard_map/pallas_call | solution.py:531
  54.8 0.0 copy-start
  54.8 11.6 %shard_map.127.refs_3_ = f32[1,2,512,512]{3,2,1,0:T(8,128)S(1)} custom-call(f32[2,512,512]{2,1,0:T(8,128)S(1)} %shard_map.126.in_ref.refs_2_), custom_call_target="tpu_custom_call" | custom-call | tf_op jit(solution)/shard_map/pallas_call | solution.py:534
  66.4 0.0 copy-done
  66.4 0.0 copy-start.2
  66.4 0.0 copy-start.4
  66.5 0.0 copy-start.5
  66.5 5.1 %shard_map.128 = (f32[2,512,512]{2,1,0:T(8,128)}, f32[32,64,128]{2,1,0:T(8,128)S(1)}) custom-call(s32[1]{0:T(128)} %bitcast.refs_0_.me_ref, s32[16,128]{1,0:T(8,128)S(1)} %bitcast.28, f32[2,512,512]{2,1,0:T(8,128)S(1)} %shard_map.126.in_ref.refs_2_, f32[1,2,512,512]{3,2,1,0:T(8,128)S(1)} %shard_map.127.refs_3_, f32[512,512]{1,0:T(8,128)S(1)} %copy-done), custom_call_target="tpu_custom_call" | custom-call | tf_op jit(solution)/shard_map/pallas_call | solution.py:537
  71.6 15.0 %shard_map.129.got_ref = f32[16,64,128]{2,1,0:T(8,128)S(1)} custom-call(f32[32,64,128]{2,1,0:T(8,128)S(1)} %get-tuple-element.13.refs_0_.mine_ref), custom_call_target="tpu_custom_call" | custom-call | tf_op jit(solution)/shard_map/pallas_call | solution.py:525
  86.6 0.0 copy-done.2
  86.6 0.0 copy-done.4
  86.6 0.0 copy-done.5
  86.6 7.9 %shard_map.130 = f32[16,1024]{1,0:T(8,128)} custom-call(s32[1]{0:T(128)} %bitcast.refs_0_.me_ref, s32[16,128]{1,0:T(8,128)S(1)} %bitcast.29, s32[16]{0:T(128)S(1)} %get-tuple-element.11.where_ref, f32[16,64,128]{2,1,0:T(8,128)S(1)} %shard_map.129.got_ref, f32[32,64,128]{2,1,0:T(8,128)S(1)} %get-tuple-element.13.refs_0_.mine_ref, ...), custom_call_target="tpu_custom_call" | custom-call | tf_op jit(solution)/shard_map/pallas_call | solution.py:542
  (5 shorter events, 0.1 us)
Async XLA Ops:
  0.6 40.4 %copy-start.6 = (bf16[256,256]{1,0:T(8,128)(2,1)S(1)}, bf16[256,256]{1,0:T(8,128)(2,1)}, u32[]{:S(2)}) copy-start(bf16[256,256]{1,0:T(8,128)(2,1)} %constant.68.clone.refs_5_) | copy-start | bytes 393220
  12.0 0.8 copy-start.1
  12.8 0.8 copy-start.7
  41.0 0.8 copy-start.3
  54.8 11.7 %copy-start = (f32[512,512]{1,0:T(8,128)S(1)}, f32[512,512]{1,0:T(8,128)}, u32[]{:S(2)}) copy-start(f32[512,512]{1,0:T(8,128)} %refs_4_.2) | copy-start | bytes 3145732
  66.4 20.1 %copy-start.2 = (f32[1,16,1024]{2,1,0:T(8,128)S(1)}, f32[1,16,1024]{2,1,0:T(8,128)}, u32[]{:S(2)}) copy-start(f32[1,16,1024]{2,1,0:T(8,128)} %param.12) | copy-start | bytes 196612
  66.4 20.1 %copy-start.4 = (bf16[128,256]{1,0:T(8,128)(2,1)S(1)}, bf16[128,256]{1,0:T(8,128)(2,1)}, u32[]{:S(2)}) copy-start(bf16[128,256]{1,0:T(8,128)(2,1)} %constant.67.clone.refs_4_.left_ref) | copy-start | bytes 196612
  66.5 20.1 %copy-start.5 = (bf16[256,256]{1,0:T(8,128)(2,1)S(1)}, bf16[256,256]{1,0:T(8,128)(2,1)}, u32[]{:S(2)}) copy-start(bf16[256,256]{1,0:T(8,128)(2,1)} %constant.69.clone.right_ref) | copy-start | bytes 393220

commit v3 on v2

--- a/solution.py
+++ b/solution.py
@@ -122,7 +122,7 @@
     return [m[i * S : (i + 1) * S] for i in range(len(blocks))]
 
 
-def make_images(vis_ref, coord_ref, out_ref):
+def make_images(vis_ref, coord_ref, out_ref, wave_ref, trig_ref):
     rows = vis_ref.shape[1] // 2
 
     def step(b, _):
@@ -130,7 +130,13 @@
         cu, su = phases(coord_ref[at, :rows])
         cv, sv = phases(coord_ref[at, rows:])
         vr, vi = vis_ref[at, :rows], vis_ref[at, rows:]
+        trig_ref[b, :S] = cv
+        trig_ref[b, S:] = sv
         ahi, alo = split(jnp.concatenate([cu, su], 0))
+        wave_ref[b, :S, :rows] = ahi[:S]
+        wave_ref[b, :S, rows:] = ahi[S:]
+        wave_ref[b, S:, :rows] = alo[:S]
+        wave_ref[b, S:, rows:] = alo[S:]
         bhi, blo = split(jnp.concatenate([vr * cv - vi * sv, vr * sv + vi * cv], 0))
         m = lax.dot_general(
             jnp.concatenate([ahi, alo], 0),
@@ -227,38 +233,48 @@
     lax.fori_loop(0, info_ref[me, 5 * NB], own, 0)
 
 
-def tile_kernel(n_vert, n_au, me_ref, info_ref, got_ref, mine_ref, out_ref, pad_ref):
+def tile_kernel(n_vert, n_au, me_ref, info_ref, got_ref, mine_ref, out_ref, meta_ref, pad_ref):
+    def clear(i, _):
+        meta_ref[i] = 0
+        return 0
+
+    lax.fori_loop(0, 3 * NSLOT, clear, 0)
+
+    def note(slot, row_at, col_at):
+        meta_ref[slot] = row_at
+        meta_ref[NSLOT + slot] = col_at
+        meta_ref[2 * NSLOT + slot] = 1
+
+    incoming(n_vert, n_au, me_ref[0], info_ref, note)
     pad_ref[...] = jnp.zeros_like(pad_ref)
     low = low_half((S, 2 * S))
     blank = jnp.zeros((S, 2 * S), F32)
     blank_rows = jnp.zeros((8, 256), F32)
 
-    def visit(slot, row_at, col_at):
-        top = pl.multiple_of(row_at // 8 * 8, 8)
-        start = pl.multiple_of(col_at // 128 * 128, 128)
-        shift = col_at % 128
-
-        def put(x):
-            for plane in range(2):
-                part = x if plane == 0 else pltpu.roll(x, S, 1)
-                wide = jnp.concatenate([jnp.where(low, part, 0.0), blank], 1)
-                wide = jnp.concatenate([pltpu.roll(wide, shift, 1), blank_rows], 0)
-                at = (plane, pl.ds(top, S + 8), pl.ds(start, 256))
-                pad_ref[at] += pltpu.roll(wide, row_at % 8, 0)
-
-        @pl.when(slot < NR * CAP)
-        def _():
-            put(got_ref[jnp.minimum(slot, NR * CAP - 1)])
-
-        @pl.when(slot >= NR * CAP)
-        def _():
-            put(mine_ref[slot])
-
-    incoming(n_vert, n_au, me_ref[0], info_ref, visit)
+    def add_all(ref, base, count):
+        def step(i, _):
+            for j in range(2):
+                slot = base + i * 2 + j
+                row_at, col_at = meta_ref[slot], meta_ref[NSLOT + slot]
+                x = jnp.where(meta_ref[2 * NSLOT + slot] > 0, ref[slot], 0.0)
+                top = pl.multiple_of(row_at // 8 * 8, 8)
+                start = pl.multiple_of(col_at // 128 * 128, 128)
+                for plane in range(2):
+                    part = x if plane == 0 else pltpu.roll(x, S, 1)
+                    wide = jnp.concatenate([jnp.where(low, part, 0.0), blank], 1)
+                    wide = jnp.concatenate([pltpu.roll(wide, col_at % 128, 1), blank_rows], 0)
+                    at = (plane, pl.ds(top, S + 8), pl.ds(start, 256))
+                    pad_ref[at] += pltpu.roll(wide, row_at % 8, 0)
+            return 0
+
+        lax.fori_loop(0, count // 2, step, 0)
+
+    add_all(got_ref, 0, NR * CAP)
+    add_all(mine_ref, NR * CAP, NB)
     out_ref[...] = pad_ref[:, :TS, :TS]
 
 
-def window_kernel(n_vert, n_au, me_ref, info_ref, tile_ref, other_ref, taper_ref, model_ref, win_ref, pad_ref):
+def window_kernel(meta_ref, tile_ref, other_ref, taper_ref, model_ref, win_ref, pad_ref):
     total = tile_ref[...]
     for k in range(other_ref.shape[0]):
         total = total + other_ref[k]
@@ -269,7 +285,8 @@
     pad_ref[:, TS:, :] = jnp.zeros((2, 8, TS + 128), F32)
     low = low_half((S, 2 * S))
 
-    def visit(slot, row_at, col_at):
+    def cut(slot):
+        row_at, col_at = meta_ref[slot], meta_ref[NSLOT + slot]
         top = pl.multiple_of(row_at // 8 * 8, 8)
         lift = lax.rem(S + 8 - row_at % 8, S + 8)
         start = pl.multiple_of(col_at // 128 * 128, 128)
@@ -279,14 +296,20 @@
             wide = pad_ref[plane, pl.ds(top, S + 8), pl.ds(start, 256)]
             wide = pltpu.roll(wide, shift, 1)[:, : 2 * S]
             parts.append(pltpu.roll(wide, lift, 0)[:S])
-        win_ref[slot] = jnp.where(low, parts[0], pltpu.roll(parts[1], S, 1))
-
-    incoming(n_vert, n_au, me_ref[0], info_ref, visit)
-
-
-def degrid_kernel(me_ref, info_ref, where_ref, got_ref, mine_ref, aterm_ref, coord_ref, left_ref, right_ref,
-                  out_ref, win_ref):
-    rows = coord_ref.shape[1] // 2
+        return jnp.where(low, parts[0], pltpu.roll(parts[1], S, 1))
+
+    def step(i, _):
+        found = [cut(i * 2 + j) for j in range(2)]
+        for j in range(2):
+            win_ref[i * 2 + j] = found[j]
+        return 0
+
+    lax.fori_loop(0, NSLOT // 2, step, 0)
+
+
+def degrid_kernel(me_ref, info_ref, where_ref, got_ref, mine_ref, aterm_ref, wave_ref, trig_ref, left_ref,
+                  right_ref, out_ref, win_ref):
+    rows = trig_ref.shape[2]
     live = info_ref[me_ref[0], 5 * NB]
 
     def fetch(b, _):
@@ -317,10 +340,8 @@
         back = win_ref[b]
         hi = back.astype(BF).astype(F32)
         both = jnp.concatenate([hi, back - hi], 0).T.astype(BF)
-        at = pl.ds(b, 1)
-        cu, su = phases(coord_ref[at, :rows])
-        cv, sv = phases(coord_ref[at, rows:])
-        ehi, elo = split(jnp.concatenate([cu, su], 1))
+        ehi, elo = wave_ref[b, :S], wave_ref[b, S:]
+        cv, sv = trig_ref[b, :S], trig_ref[b, S:]
         m = jnp.dot(
             jnp.concatenate([both, both], 1),
             jnp.concatenate([ehi, ehi, elo, elo], 0),
@@ -367,7 +388,7 @@
 
 
 def beam_exchange_kernel(n_vert, cap, ids_ref, beam_ref, vis_ref, coord_ref, out_ref, image_ref,
-                         send_ref, send_sem, recv_sem, own_sem):
+                         wave_ref, trig_ref, send_ref, send_sem, recv_sem, own_sem):
     n = out_ref.shape[0]
     me = lax.axis_index("au") * n_vert + lax.axis_index("vert")
     barrier = pltpu.get_barrier_semaphore()
@@ -394,7 +415,7 @@
             send_ref.at[k], out_ref.at[k], send_sem.at[k], recv_sem.at[k],
             device_id=peer(k), device_id_type=MESH))
         copies[-1].start()
-    make_images(vis_ref, coord_ref, image_ref)
+    make_images(vis_ref, coord_ref, image_ref, wave_ref, trig_ref)
     own.wait()
     for copy in copies:
         copy.wait()
@@ -506,12 +527,13 @@
     order = jnp.sum((hit[:, None, :] & (entry[None, :] < entry[:, None])[None]).astype(jnp.int32), axis=2)
     pick = hit[:, None, :] & (order[:, None, :] == jnp.arange(cap, dtype=jnp.int32)[None, :, None])
     ids = jnp.sum(jnp.where(pick, (asked % per_dev)[:, None, :], 0), axis=2).reshape(n * cap)
-    found, images = remote_call(
+    found, images, waves, trigs = remote_call(
         lambda *refs: beam_exchange_kernel(n_vert, cap, *refs), 1, [SMEM] + [VMEM] * 3,
-        [shape(n, cap * S, 2 * S, dtype=BF), shape(NB, S, 2 * S)],
+        [shape(n, cap * S, 2 * S, dtype=BF), shape(NB, S, 2 * S),
+         shape(NB, 2 * S, rows2, dtype=BF), shape(NB, 2 * S, rows2 // 2)],
         [pltpu.VMEM((n, cap * S, 2 * S), BF), pltpu.SemaphoreType.DMA((n,)),
          pltpu.SemaphoreType.DMA((n,)), pltpu.SemaphoreType.DMA],
-        out_specs=[ANY, VMEM],
+        out_specs=[ANY, VMEM, VMEM, VMEM],
     )(ids, beams[0].reshape(per_dev, S, 2 * S), signal, places)
 
     subgrids, aterms, slots = local_call(
@@ -528,20 +550,21 @@
             [pltpu.SemaphoreType.DMA((NR,)), pltpu.SemaphoreType.DMA((NR,))])(values)
 
     arrived = routed(subgrids, 1, 2)
-    tile = local_call(
-        lambda *refs: tile_kernel(n_vert, n_au, *refs), [SMEM, SMEM, VMEM, VMEM], VMEM,
-        shape(2, TS, TS), [pltpu.VMEM((2, TS + 8, TS + 128), F32)])(mine, info, arrived, subgrids)
+    tile, meta = local_call(
+        lambda *refs: tile_kernel(n_vert, n_au, *refs), [SMEM, SMEM, VMEM, VMEM], [VMEM, SMEM],
+        [shape(2, TS, TS), shape(3 * NSLOT, dtype=jnp.int32)],
+        [pltpu.VMEM((2, TS + 8, TS + 128), F32)])(mine, info, arrived, subgrids)
     others = remote_call(
         tile_exchange_kernel, 3, [ANY], shape(n_af - 1, 2, TS, TS),
         [pltpu.SemaphoreType.DMA((n_af - 1,)), pltpu.SemaphoreType.DMA((n_af - 1,))])(tile)
     model_grid, windows = local_call(
-        lambda *refs: window_kernel(n_vert, n_au, *refs), [SMEM, SMEM] + [VMEM] * 3, [VMEM, VMEM],
+        window_kernel, [SMEM] + [VMEM] * 3, [VMEM, VMEM],
         [shape(2, TS, TS), shape(NSLOT, S, 2 * S)], [pltpu.VMEM((2, TS + 8, TS + 128), F32)],
-    )(mine, info, tile, others, taper)
+    )(meta, tile, others, taper)
     returned = routed(windows, -1, 4)
     result = local_call(
-        degrid_kernel, [SMEM] * 3 + [VMEM] * 6, VMEM, shape(NB, rows2), [pltpu.VMEM((NB, S, 2 * S), F32)],
-    )(mine, info, slots, returned, windows, aterms, places, left, right_conj)
+        degrid_kernel, [SMEM] * 3 + [VMEM] * 7, VMEM, shape(NB, rows2), [pltpu.VMEM((NB, S, 2 * S), F32)],
+    )(mine, info, slots, returned, windows, aterms, waves, trigs, left, right_conj)
     return (result[None], model_grid)
 
 

time: 96.1 us -> 94.3 us (0.981); the launches traced: 94.5 us -> 94 us
    pallas_call x1, Pallas kernels: 3.98 us -> 6.73 us  [body(): local_call(lambda *refs: tile_kernel(n_vert, n_au, *refs), [SMEM, SMEM, V...]
    pallas_call x1, Pallas kernels: 11.6 us -> 9.87 us  [body(): remote_call(tile_exchange_kernel, 3, [ANY], shape(n_af - 1, 2, TS, TS), [...]
    unnamed x17 -> x15, local copies, waits for them, and re-layouts: 3.7 us -> 3.7 us
where the time goes in v3:
time: 94.3 us; the launch traced here: 94 us
  Pallas kernels  86.2 us (91%)
  local copies, waits for them, and re-layouts  5.68 us (6%)
  between operations  1.52 us (2%)
    pallas_call x1, Pallas kernels, body(): remote_call(lambda *refs: beam_exchange_kernel(n_vert, cap, *refs), 1, [S...  27.3 us
    pallas_call x2, Pallas kernels, routed(): remote_call(lambda *refs: route_kernel(n_au, n_vert, sign, *refs), ident,...  19.5 us
    pallas_call x1, Pallas kernels, body(): remote_call(tile_exchange_kernel, 3, [ANY], shape(n_af - 1, 2, TS, TS), [...  9.87 us
    pallas_call x1, Pallas kernels, body(): remote_call(lambda *refs: info_kernel(n_vert, *refs), 5, [VMEM], shape(n,...  6.89 us
    pallas_call x1, Pallas kernels, body(): local_call(lambda *refs: tile_kernel(n_vert, n_au, *refs), [SMEM, SMEM, V...  6.73 us
    pallas_call x1, Pallas kernels, body(): local_call(degrid_kernel, [SMEM] * 3 + [VMEM] * 7, VMEM, shape(NB, rows2)...  6.71 us
    pallas_call x1, Pallas kernels, body(): local_call(window_kernel, [SMEM] + [VMEM] * 3, [VMEM, VMEM], [shape(2, TS...  5.4 us
    pallas_call x1, Pallas kernels, body(): local_call(lambda *refs: subgrid_kernel(n_vert, per_dev, cap, *refs), [SM...  3.73 us

profile of v3, /device:TPU:9, one launch (start us, length us, event | category | flops | bytes accessed | tf_op | source)
XLA Modules:
  0.0 94.0 jit_solution(2920329227248126791)
XLA Ops:
  0.6 0.0 copy-start.4
  1.4 0.8 slice_bitcast_fusion
  2.1 0.7 concatenate.7
  2.9 6.9 %shard_map.122 = s32[16,1,128]{2,1,0:T(1,128)S(1)} custom-call(s32[1,128]{1,0:T(1,128)S(1)} %bitcast.31), custom_call_target="tpu_custom_call" | custom-call | tf_op jit(solution)/shard_map/pallas_call | solution.py:516
  9.8 0.1 slice.20
  9.9 0.1 reshape.91
  9.9 0.1 copy.25
  10.0 0.1 copy.26
  10.1 0.3 convert_reduce_fusion
  10.5 0.1 select_reduce_fusion
  10.6 0.1 copy.30
  10.7 0.1 reshape.93.refs_0_
  10.8 1.2 %copy.31 = bf16[4,8,64,128]{3,2,1,0:T(8,128)(2,1)S(1)} copy(bf16[4,8,64,128]{3,1,2,0:T(8,128)(2,1)} %bitcast.32) | data formatting | bytes 1048576
  12.0 0.0 copy-start.5
  12.0 0.8 copy-done.5
  12.8 0.0 copy-start.6
  12.8 0.8 copy-done.6
  13.7 27.3 %shard_map.123 = (bf16[16,256,128]{2,1,0:T(8,128)(2,1)S(1)}, f32[16,64,128]{2,1,0:T(8,128)S(1)}, bf16[16,128,1024]{2,1,0:T(8,128)(2,1)S(1)}, f32[16,128,512]{2,1,0:T(8,128)S(1)}) custom-call(s32[64]{0:T(128)S(1)} %reshape.93.refs_0_, bf16[32,64,128]{2,1,0:T(8,128)(2,1)S(1)} %bitcast.23, f32[16,1024]{1,0:T(8,128)S(1)} %bitcast.29, f32[16,1024]{1,0:T(8,128)S(1)} %bitcast.30), custom_call_target="tpu_custom_call" | custom-call | tf_op jit(solution)/shard_map/pallas_call | solution.py:530
  41.0 0.0 copy-done.4
  41.0 0.0 copy-start.1
  41.0 0.8 copy-done.1
  41.9 3.7 %shard_map.124 = (f32[32,64,128]{2,1,0:T(8,128)S(1)}, f32[16,64,128]{2,1,0:T(8,128)S(1)}, s32[16]{0:T(128)S(1)}) custom-call(s32[1]{0:T(128)} %bitcast.refs_0_.me_ref, s32[16,128]{1,0:T(8,128)S(1)} %bitcast.26, f32[16,64,128]{2,1,0:T(8,128)S(1)} %get-tuple-element.13.refs_2_, bf16[64,64,128]{2,1,0:T(8,128)(2,1)S(1)} %bitcast.24, ...), custom_call_target="tpu_custom_call" | custom-call | tf_op jit(solution)/shard_map/pallas_call | solution.py:539
  45.6 5.2 %shard_map.125.refs_2_ = f32[16,64,128]{2,1,0:T(8,128)S(1)} custom-call(f32[32,64,128]{2,1,0:T(8,128)S(1)} %get-tuple-element.16.refs_0_.refs_3_), custom_call_target="tpu_custom_call" | custom-call | tf_op jit(solution)/shard_map/pallas_call | solution.py:547
  50.8 6.7 %shard_map.126 = (f32[2,512,512]{2,1,0:T(8,128)S(1)}, s32[96]{0:T(128)S(1)}) custom-call(s32[1]{0:T(128)} %bitcast.refs_0_.me_ref, s32[16,128]{1,0:T(8,128)S(1)} %bitcast.27, f32[16,64,128]{2,1,0:T(8,128)S(1)} %shard_map.125.refs_2_, f32[32,64,128]{2,1,0:T(8,128)S(1)} %get-tuple-element.16.refs_0_.refs_3_), custom_call_target="tpu_custom_call" | custom-call | tf_op jit(solution)/shard_map/pallas_call | solution.py:553
  57.5 0.0 copy-start
  57.5 9.9 %shard_map.127.other_ref = f32[1,2,512,512]{3,2,1,0:T(8,128)S(1)} custom-call(f32[2,512,512]{2,1,0:T(8,128)S(1)} %get-tuple-element.18.in_ref.tile_ref), custom_call_target="tpu_custom_call" | custom-call | tf_op jit(solution)/shard_map/pallas_call | solution.py:557
  67.4 0.0 copy-done
  67.4 0.0 copy-start.2
  67.4 0.0 copy-start.3
  67.4 5.4 %shard_map.128 = (f32[2,512,512]{2,1,0:T(8,128)}, f32[32,64,128]{2,1,0:T(8,128)S(1)}) custom-call(s32[96]{0:T(128)S(1)} %get-tuple-element.17.meta_ref, f32[2,512,512]{2,1,0:T(8,128)S(1)} %get-tuple-element.18.in_ref.tile_ref, f32[1,2,512,512]{3,2,1,0:T(8,128)S(1)} %shard_map.127.other_ref, f32[512,512]{1,0:T(8,128)S(1)} %copy-done), custom_call_target="tpu_custom_call" | custom-call | tf_op jit(solution)/shard_map/pallas_call | solution.py:560
  72.8 14.4 %shard_map.129.got_ref = f32[16,64,128]{2,1,0:T(8,128)S(1)} custom-call(f32[32,64,128]{2,1,0:T(8,128)S(1)} %get-tuple-element.19.refs_0_.mine_ref), custom_call_target="tpu_custom_call" | custom-call | tf_op jit(solution)/shard_map/pallas_call | solution.py:547
  87.2 0.0 copy-done.2
  87.2 0.0 copy-done.3
  87.3 6.7 %shard_map.130 = f32[16,1024]{1,0:T(8,128)} custom-call(s32[1]{0:T(128)} %bitcast.refs_0_.me_ref, s32[16,128]{1,0:T(8,128)S(1)} %bitcast.28, s32[16]{0:T(128)S(1)} %get-tuple-element.15.where_ref, f32[16,64,128]{2,1,0:T(8,128)S(1)} %shard_map.129.got_ref, f32[32,64,128]{2,1,0:T(8,128)S(1)} %get-tuple-element.19.refs_0_.mine_ref, ...), custom_call_target="tpu_custom_call" | custom-call | tf_op jit(solution)/shard_map/pallas_call | solution.py:565
  (5 shorter events, 0.1 us)
Async XLA Ops:
  0.6 40.4 %copy-start.4 = (bf16[256,256]{1,0:T(8,128)(2,1)S(1)}, bf16[256,256]{1,0:T(8,128)(2,1)}, u32[]{:S(2)}) copy-start(bf16[256,256]{1,0:T(8,128)(2,1)} %constant.68.clone.refs_5_) | copy-start | bytes 393220
  12.0 0.8 copy-start.5
  12.8 0.8 copy-start.6
  41.0 0.8 copy-start.1
  57.5 9.9 %copy-start = (f32[512,512]{1,0:T(8,128)S(1)}, f32[512,512]{1,0:T(8,128)}, u32[]{:S(2)}) copy-start(f32[512,512]{1,0:T(8,128)} %taper_ref.1) | copy-start | bytes 3145732
  67.4 19.8 %copy-start.2 = (bf16[128,256]{1,0:T(8,128)(2,1)S(1)}, bf16[128,256]{1,0:T(8,128)(2,1)}, u32[]{:S(2)}) copy-start(bf16[128,256]{1,0:T(8,128)(2,1)} %constant.67.clone.refs_4_.left_ref) | copy-start | bytes 196612
  67.4 19.8 %copy-start.3 = (bf16[256,256]{1,0:T(8,128)(2,1)S(1)}, bf16[256,256]{1,0:T(8,128)(2,1)}, u32[]{:S(2)}) copy-start(bf16[256,256]{1,0:T(8,128)(2,1)} %constant.69.clone.right_ref) | copy-start | bytes 393220

commit v4 on v3

--- a/solution.py
+++ b/solution.py
@@ -410,7 +410,7 @@
     own.start()
     pl.semaphore_wait(barrier, n - 1)
     copies = []
-    for k in range(1, n):
+    for k in sorted(range(1, n), key=lambda k: -min(k % n_vert, -k % n_vert)):
         copies.append(pltpu.make_async_remote_copy(
             send_ref.at[k], out_ref.at[k], send_sem.at[k], recv_sem.at[k],
             device_id=peer(k), device_id_type=MESH))

time: 94.3 us -> 95.6 us (1.014)
  Pallas kernels: 86.2 us -> 87.5 us
    pallas_call x1, Pallas kernels: 27.3 us -> 28.6 us  [body(): remote_call(lambda *refs: beam_exchange_kernel(n_vert, cap, *refs), 1, [S...]
where the time goes in v4:
time: 95.6 us; the launch traced here: 95.2 us
  Pallas kernels  87.5 us (92%)
  local copies, waits for them, and re-layouts  5.68 us (6%)
  between operations  1.52 us (2%)
    pallas_call x1, Pallas kernels, body(): remote_call(lambda *refs: beam_exchange_kernel(n_vert, cap, *refs), 1, [S...  28.6 us
    pallas_call x2, Pallas kernels, routed(): remote_call(lambda *refs: route_kernel(n_au, n_vert, sign, *refs), ident,...  19.5 us
    pallas_call x1, Pallas kernels, body(): remote_call(tile_exchange_kernel, 3, [ANY], shape(n_af - 1, 2, TS, TS), [...  9.86 us
    pallas_call x1, Pallas kernels, body(): remote_call(lambda *refs: info_kernel(n_vert, *refs), 5, [VMEM], shape(n,...  6.89 us
    pallas_call x1, Pallas kernels, body(): local_call(lambda *refs: tile_kernel(n_vert, n_au, *refs), [SMEM, SMEM, V...  6.73 us
    pallas_call x1, Pallas kernels, body(): local_call(degrid_kernel, [SMEM] * 3 + [VMEM] * 7, VMEM, shape(NB, rows2)...  6.72 us
    pallas_call x1, Pallas kernels, body(): local_call(window_kernel, [SMEM] + [VMEM] * 3, [VMEM, VMEM], [shape(2, TS...  5.4 us
    pallas_call x1, Pallas kernels, body(): local_call(lambda *refs: subgrid_kernel(n_vert, per_dev, cap, *refs), [SM...  3.74 us

profile of v4, /device:TPU:9, one launch (start us, length us, event | category | flops | bytes accessed | tf_op | source)
XLA Modules:
  0.0 95.2 jit_solution(12597522376910245988)
XLA Ops:
  0.6 0.0 copy-start.4
  1.4 0.8 slice_bitcast_fusion
  2.1 0.7 concatenate.7
  2.9 6.9 %shard_map.122 = s32[16,1,128]{2,1,0:T(1,128)S(1)} custom-call(s32[1,128]{1,0:T(1,128)S(1)} %bitcast.31), custom_call_target="tpu_custom_call" | custom-call | tf_op jit(solution)/shard_map/pallas_call | solution.py:516
  9.8 0.1 slice.20
  9.9 0.1 reshape.91
  9.9 0.1 copy.25
  10.0 0.1 copy.26
  10.1 0.3 convert_reduce_fusion
  10.5 0.1 select_reduce_fusion
  10.6 0.1 copy.30
  10.7 0.1 reshape.93.refs_0_
  10.8 1.2 %copy.31 = bf16[4,8,64,128]{3,2,1,0:T(8,128)(2,1)S(1)} copy(bf16[4,8,64,128]{3,1,2,0:T(8,128)(2,1)} %bitcast.32) | data formatting | bytes 1048576
  12.0 0.0 copy-start.5
  12.0 0.8 copy-done.5
  12.8 0.0 copy-start.6
  12.8 0.8 copy-done.6
  13.7 28.6 %shard_map.123 = (bf16[16,256,128]{2,1,0:T(8,128)(2,1)S(1)}, f32[16,64,128]{2,1,0:T(8,128)S(1)}, bf16[16,128,1024]{2,1,0:T(8,128)(2,1)S(1)}, f32[16,128,512]{2,1,0:T(8,128)S(1)}) custom-call(s32[64]{0:T(128)S(1)} %reshape.93.refs_0_, bf16[32,64,128]{2,1,0:T(8,128)(2,1)S(1)} %bitcast.23, f32[16,1024]{1,0:T(8,128)S(1)} %bitcast.29, f32[16,1024]{1,0:T(8,128)S(1)} %bitcast.30), custom_call_target="tpu_custom_call" | custom-call | tf_op jit(solution)/shard_map/pallas_call | solution.py:530
  42.3 0.0 copy-done.4
  42.3 0.0 copy-start.1
  42.3 0.8 copy-done.1
  43.2 3.7 %shard_map.124 = (f32[32,64,128]{2,1,0:T(8,128)S(1)}, f32[16,64,128]{2,1,0:T(8,128)S(1)}, s32[16]{0:T(128)S(1)}) custom-call(s32[1]{0:T(128)} %bitcast.refs_0_.me_ref, s32[16,128]{1,0:T(8,128)S(1)} %bitcast.26, f32[16,64,128]{2,1,0:T(8,128)S(1)} %get-tuple-element.13.refs_2_, bf16[64,64,128]{2,1,0:T(8,128)(2,1)S(1)} %bitcast.24, ...), custom_call_target="tpu_custom_call" | custom-call | tf_op jit(solution)/shard_map/pallas_call | solution.py:539
  46.9 5.1 %shard_map.125.refs_2_ = f32[16,64,128]{2,1,0:T(8,128)S(1)} custom-call(f32[32,64,128]{2,1,0:T(8,128)S(1)} %get-tuple-element.16.refs_0_.refs_3_), custom_call_target="tpu_custom_call" | custom-call | tf_op jit(solution)/shard_map/pallas_call | solution.py:547
  52.1 6.7 %shard_map.126 = (f32[2,512,512]{2,1,0:T(8,128)S(1)}, s32[96]{0:T(128)S(1)}) custom-call(s32[1]{0:T(128)} %bitcast.refs_0_.me_ref, s32[16,128]{1,0:T(8,128)S(1)} %bitcast.27, f32[16,64,128]{2,1,0:T(8,128)S(1)} %shard_map.125.refs_2_, f32[32,64,128]{2,1,0:T(8,128)S(1)} %get-tuple-element.16.refs_0_.refs_3_), custom_call_target="tpu_custom_call" | custom-call | tf_op jit(solution)/shard_map/pallas_call | solution.py:553
  58.8 0.0 copy-start
  58.8 9.9 %shard_map.127.other_ref = f32[1,2,512,512]{3,2,1,0:T(8,128)S(1)} custom-call(f32[2,512,512]{2,1,0:T(8,128)S(1)} %get-tuple-element.18.in_ref.tile_ref), custom_call_target="tpu_custom_call" | custom-call | tf_op jit(solution)/shard_map/pallas_call | solution.py:557
  68.7 0.0 copy-done
  68.7 0.0 copy-start.2
  68.7 0.0 copy-start.3
  68.7 5.4 %shard_map.128 = (f32[2,512,512]{2,1,0:T(8,128)}, f32[32,64,128]{2,1,0:T(8,128)S(1)}) custom-call(s32[96]{0:T(128)S(1)} %get-tuple-element.17.meta_ref, f32[2,512,512]{2,1,0:T(8,128)S(1)} %get-tuple-element.18.in_ref.tile_ref, f32[1,2,512,512]{3,2,1,0:T(8,128)S(1)} %shard_map.127.other_ref, f32[512,512]{1,0:T(8,128)S(1)} %copy-done), custom_call_target="tpu_custom_call" | custom-call | tf_op jit(solution)/shard_map/pallas_call | solution.py:560
  74.1 14.4 %shard_map.129.got_ref = f32[16,64,128]{2,1,0:T(8,128)S(1)} custom-call(f32[32,64,128]{2,1,0:T(8,128)S(1)} %get-tuple-element.19.refs_0_.mine_ref), custom_call_target="tpu_custom_call" | custom-call | tf_op jit(solution)/shard_map/pallas_call | solution.py:547
  88.5 0.0 copy-done.2
  88.5 0.0 copy-done.3
  88.5 6.7 %shard_map.130 = f32[16,1024]{1,0:T(8,128)} custom-call(s32[1]{0:T(128)} %bitcast.refs_0_.me_ref, s32[16,128]{1,0:T(8,128)S(1)} %bitcast.28, s32[16]{0:T(128)S(1)} %get-tuple-element.15.where_ref, f32[16,64,128]{2,1,0:T(8,128)S(1)} %shard_map.129.got_ref, f32[32,64,128]{2,1,0:T(8,128)S(1)} %get-tuple-element.19.refs_0_.mine_ref, ...), custom_call_target="tpu_custom_call" | custom-call | tf_op jit(solution)/shard_map/pallas_call | solution.py:565
  (5 shorter events, 0.1 us)
Async XLA Ops:
  0.6 41.7 %copy-start.4 = (bf16[256,256]{1,0:T(8,128)(2,1)S(1)}, bf16[256,256]{1,0:T(8,128)(2,1)}, u32[]{:S(2)}) copy-start(bf16[256,256]{1,0:T(8,128)(2,1)} %constant.68.clone.refs_5_) | copy-start | bytes 393220
  12.0 0.8 copy-start.5
  12.8 0.8 copy-start.6
  42.3 0.8 copy-start.1
  58.8 9.9 %copy-start = (f32[512,512]{1,0:T(8,128)S(1)}, f32[512,512]{1,0:T(8,128)}, u32[]{:S(2)}) copy-start(f32[512,512]{1,0:T(8,128)} %taper_ref.1) | copy-start | bytes 3145732
  68.7 19.8 %copy-start.2 = (bf16[128,256]{1,0:T(8,128)(2,1)S(1)}, bf16[128,256]{1,0:T(8,128)(2,1)}, u32[]{:S(2)}) copy-start(bf16[128,256]{1,0:T(8,128)(2,1)} %constant.67.clone.refs_4_.left_ref) | copy-start | bytes 196612
  68.7 19.8 %copy-start.3 = (bf16[256,256]{1,0:T(8,128)(2,1)S(1)}, bf16[256,256]{1,0:T(8,128)(2,1)}, u32[]{:S(2)}) copy-start(bf16[256,256]{1,0:T(8,128)(2,1)} %constant.69.clone.right_ref) | copy-start | bytes 393220
